TPU v7x, 32 devices: a whole 2x2x4 slice. The times are simulated.
32 devices in a mesh: row: 8 (over z, x), col: 4 (over y, core).
Axes of the slice: x: 2, y: 2, z: 4, core: 2. Of those that a mesh axis runs over, the one named last changes fastest.
Arguments:
- features: bfloat16 [8192, 602], P(('row', 'col')), may hold values from -6 to 6
- adjacency: bfloat16 [8192, 8192], P('col', 'row'), may hold values from -0.09375 to 0.09375
- occupancy: int32 [16, 32], P('col', 'row'), may hold values 0 or 1
- labels: int32 [8192], P(('row', 'col')), may hold values from 0 to 40
- train_mask: int32 [8192], P(('row', 'col')), may hold values from 0 to 1, as said below
- node_count: int32 [32], P(('row', 'col')), may hold values from 129 to 256
- weight_one: float32 [602, 256], replicated, may hold values from -0.25 to 0.25
- weight_two: float32 [256, 256], replicated, may hold values from -0.375 to 0.375
- weight_three: float32 [256, 41], replicated, may hold values from -0.375 to 0.375
- biases: float32 [553], replicated, may hold values from -0.6 to 0.6
- first_one: float32 [602, 256], replicated, may hold values from -0.013671875 to 0.013671875
- first_two: float32 [256, 256], replicated, may hold values from -0.013671875 to 0.013671875
- first_three: float32 [256, 41], replicated, may hold values from -0.013671875 to 0.013671875
- first_bias: float32 [553], replicated, may hold values from -0.013671875 to 0.013671875
- second_one: float32 [602, 256], replicated, as said below
- second_two: float32 [256, 256], replicated, as said below
- second_three: float32 [256, 41], replicated, as said below
- second_bias: float32 [553], replicated, as said below
Outputs:
- new_first_one: float32 [602, 256], replicated
- new_second_one: float32 [602, 256], replicated
- new_weight_one: float32 [602, 256], replicated
- new_first_two: float32 [256, 256], replicated
- new_second_two: float32 [256, 256], replicated
- new_weight_two: float32 [256, 256], replicated
- new_first_three: float32 [256, 41], replicated
- new_second_three: float32 [256, 41], replicated
- new_weight_three: float32 [256, 41], replicated
- new_first_bias: float32 [553], replicated
- new_second_bias: float32 [553], replicated
- new_biases: float32 [553], replicated
- loss_sum: float32 [], replicated
- train_count: float32 [], replicated
Inputs may be any that keep to these rules, and one draw needn't show every extreme that they name: `train_mask`: 0 or 1; the share of training nodes differs between blocks. `second_one`: positive. `second_two`: positive. `second_three`: positive. `second_bias`: positive.
All inputs are finite; a program needn't handle non-finite values. No bound on the sum of `occupancy` on one device may be relied on, other than what follows from the above.
Results may differ from a plain program's by a relative error of at most 0.0095.
Values may be sent and summed in bfloat16 or wider, within the bound.
A program may use at most 192 MiB of HBM per device.

v0:
```python
import jax
import jax.numpy as jnp
from jax import lax
from jax.sharding import PartitionSpec as P

SUB = 512
STEP = 5


B_ONE = 0.5
B_TWO = 0.5
RATE = 0.05
DECAY = 0.01
EPSILON = 1e-08
SMOOTH = 0.1


def adam_update(weight, first, second, grad):
    first_new = B_ONE * first + (1.0 - B_ONE) * grad
    second_new = B_TWO * second + (1.0 - B_TWO) * grad * grad
    fix_one = 1.0 - B_ONE**STEP
    fix_two = 1.0 - B_TWO**STEP
    step_size = first_new / fix_one / (jnp.sqrt(second_new / fix_two) + EPSILON) + DECAY * weight
    return (first_new, second_new, weight - RATE * step_size)


def inner_rows(left, right):
    return lax.dot_general(
        left, right, (((0,), (0,)), ((), ())), preferred_element_type=jnp.float32
    )


def shards(
    features,
    adjacency,
    occupancy,
    labels,
    train_mask,
    node_count,
    weight_one,
    weight_two,
    weight_three,
    biases,
    first_one,
    first_two,
    first_three,
    first_bias,
    second_one,
    second_two,
    second_three,
    second_bias,
):
    own = features.shape[0]
    width = weight_two.shape[0]
    classes = weight_three.shape[1]
    cover = jnp.repeat(jnp.repeat(occupancy.astype(jnp.bfloat16), SUB, axis=0), own, axis=1)
    tile = adjacency * cover
    valid = (jnp.arange(own) < node_count[0]).astype(jnp.float32)
    valid_low = valid.astype(jnp.bfloat16)[:, None]
    counted = train_mask.astype(jnp.float32) * valid
    total = lax.psum(jnp.sum(counted), ("row", "col"))
    lows = (
        weight_one.astype(jnp.bfloat16),
        weight_two.astype(jnp.bfloat16),
        weight_three.astype(jnp.bfloat16),
    )
    bias_parts = (biases[:width], biases[width : 2 * width], biases[2 * width :])
    inputs = features * valid_low
    target = (1.0 - SMOOTH) * jax.nn.one_hot(labels, classes, dtype=jnp.float32) + SMOOTH / classes

    def spread(values):
        whole = lax.all_gather(values, "col", axis=0, tiled=True)
        return lax.psum_scatter(
            jnp.dot(tile, whole, preferred_element_type=jnp.float32),
            "row",
            scatter_dimension=0,
            tiled=True,
        ) + values.astype(jnp.float32)

    def collect(grads):
        whole = lax.all_gather(grads, "row", axis=0, tiled=True)
        return lax.psum_scatter(
            inner_rows(tile, whole), "col", scatter_dimension=0, tiled=True
        ) + grads.astype(jnp.float32)

    def forward():
        hidden = inputs
        kept = []
        for layer in range(2):
            mixed = jnp.dot(hidden, lows[layer], preferred_element_type=jnp.float32).astype(
                jnp.bfloat16
            )
            summed = spread(mixed) + bias_parts[layer]
            kept.append((hidden, summed))
            hidden = jax.nn.gelu(summed).astype(jnp.bfloat16) * valid_low
        pooled = spread(hidden).astype(jnp.bfloat16)
        logits = jnp.dot(pooled, lows[2], preferred_element_type=jnp.float32) + bias_parts[2]
        return (kept, pooled, logits)

    def loss_terms(logits):
        logp = jax.nn.log_softmax(logits, axis=1)
        return (logp, jnp.sum(-jnp.sum(target * logp, axis=1) * counted))

    loss_part = loss_terms(forward()[2])[1]
    kept, pooled, logits = forward()
    logp = loss_terms(logits)[0]
    back_logits = ((jnp.exp(logp) - target) * (counted / total)[:, None]).astype(jnp.bfloat16)
    weight_grads = [None, None, inner_rows(pooled, back_logits)]
    bias_grads = [None, None, jnp.sum(back_logits.astype(jnp.float32), axis=0)]
    back_pooled = jnp.dot(back_logits, lows[2].T, preferred_element_type=jnp.float32).astype(
        jnp.bfloat16
    )
    back_hidden = collect(back_pooled) * valid[:, None]
    for layer in (1, 0):
        hidden_in, summed = kept[layer]
        back_summed = jax.vjp(jax.nn.gelu, summed)[1](back_hidden)[0].astype(jnp.bfloat16)
        bias_grads[layer] = jnp.sum(back_summed.astype(jnp.float32), axis=0)
        back_mixed = collect(back_summed).astype(jnp.bfloat16)
        weight_grads[layer] = inner_rows(hidden_in, back_mixed)
        if layer == 1:
            back_hidden = (
                jnp.dot(back_mixed, lows[1].T, preferred_element_type=jnp.float32) * valid[:, None]
            )
    grad_one, grad_two, grad_three, grad_bias, loss_sum = lax.psum(
        (weight_grads[0], weight_grads[1], weight_grads[2], jnp.concatenate(bias_grads), loss_part),
        ("row", "col"),
    )
    m_one, v_one, w_one = adam_update(weight_one, first_one, second_one, grad_one)
    m_two, v_two, w_two = adam_update(weight_two, first_two, second_two, grad_two)
    m_three, v_three, w_three = adam_update(weight_three, first_three, second_three, grad_three)
    m_bias, v_bias, w_bias = adam_update(biases, first_bias, second_bias, grad_bias)
    return (
        m_one,
        v_one,
        w_one,
        m_two,
        v_two,
        w_two,
        m_three,
        v_three,
        w_three,
        m_bias,
        v_bias,
        w_bias,
        loss_sum,
        total,
    )


def solution(mesh):
    placed = (
        P(("row", "col"), None),
        P("col", "row"),
        P("col", "row"),
        P(("row", "col")),
        P(("row", "col")),
        P(("row", "col")),
        P(),
        P(),
        P(),
        P(),
        P(),
        P(),
        P(),
        P(),
        P(),
        P(),
        P(),
        P(),
    )
    return jax.shard_map(
        shards,
        mesh=mesh,
        in_specs=placed,
        out_specs=(P(), P(), P(), P(), P(), P(), P(), P(), P(), P(), P(), P(), P(), P()),
        check_vma=False,
    )
```

profile of v0, /device:TPU:0, one launch (start us, length us, event | category | flops | bytes accessed | tf_op | source)
XLA Modules:
  0.0 672.7 jit_solution(14156627221057751131)
XLA Ops:
  8.6 2.5 broadcast_in_dim.7
  12.6 8.8 %all_gather.21 = bf16[1024,256]{1,0:T(8,128)(2,1)S(1)} all-gather(bf16[256,256]{1,0:T(8,128)(2,1)S(1)} %convolution_convert_fusion), channel_id=1, replica_groups=mesh['row'=8,'col'=4] {'col'}, dimensions={0}, use_global_device_ids=true | all-gather | bytes 655360 | tf_op jit(solution)/shard_map/all_gather | solution.py:72
  25.6 2.6 fusion.47
  28.3 68.6 %reduce-scatter.7.cloned.1.call-done = f32[256,256]{1,0:T(8,128)} async-done(((f32[2048,256]{1,0:T(8,128)}), f32[256,256]{1,0:T(8,128)}) %reduce-scatter.7.cloned.1.call-update) | async-done | bytes 262160 | tf_op jit(solution)/shard_map/reduce_scatter | solution.py:73
  98.2 7.1 %all_gather.22 = bf16[1024,256]{1,0:T(8,128)(2,1)S(1)} all-gather(bf16[256,256]{1,0:T(8,128)(2,1)S(1)} %convolution_convert_fusion.1), channel_id=1, replica_groups=mesh['row'=8,'col'=4] {'col'}, dimensions={0}, use_global_device_ids=true | all-gather | bytes 655360 | tf_op jit(solution)/shard_map/all_gather | solution.py:72
  105.3 4.8 fusion.48
  110.2 66.1 %reduce-scatter.9.cloned.1.call-done = f32[256,256]{1,0:T(8,128)} async-done(((f32[2048,256]{1,0:T(8,128)}), f32[256,256]{1,0:T(8,128)}) %reduce-scatter.9.cloned.1.call-update) | async-done | bytes 262160 | tf_op jit(solution)/shard_map/reduce_scatter | solution.py:73
  177.3 7.2 %all_gather.23 = bf16[1024,256]{1,0:T(8,128)(2,1)S(1)} all-gather(bf16[256,256]{1,0:T(8,128)(2,1)S(1)} %fusion.26), channel_id=1, replica_groups=mesh['row'=8,'col'=4] {'col'}, dimensions={0}, use_global_device_ids=true | all-gather | bytes 655360 | tf_op jit(solution)/shard_map/all_gather | solution.py:72
  184.5 4.8 fusion.49
  189.4 66.1 %reduce-scatter.11.cloned.1.call-done = f32[256,256]{1,0:T(8,128)} async-done(((f32[2048,256]{1,0:T(8,128)}), f32[256,256]{1,0:T(8,128)}) %reduce-scatter.11.cloned.1.call-update) | async-done | bytes 262160 | tf_op jit(solution)/shard_map/reduce_scatter | solution.py:73
  257.3 39.8 %psum.42 = f32[]{:T(128)} all-reduce(f32[]{:T(128)} %get-tuple-element.16), channel_id=1, replica_groups=mesh['row'=8,'col'=4] {'row','col'}, use_global_device_ids=true, to_apply=%region_6.0 | all-reduce | flops 1 | bytes 8 | tf_op jit(solution)/shard_map/psum | solution.py:61
  299.3 39.9 %all-gather.4.cloned.1.call-done = bf16[2048,256]{1,0:T(8,128)(2,1)} async-done(((bf16[256,256]{1,0:T(8,128)(2,1)}), bf16[2048,256]{1,0:T(8,128)(2,1)}) %all-gather.4.cloned.1.call-update) | async-done | bytes 1048592 | tf_op jit(solution)/shard_map/all_gather | solution.py:81
  339.2 4.7 fusion.50
  344.0 23.7 %reduce-scatter.13.cloned.1.call-done = f32[256,256]{1,0:T(8,128)} async-done(((f32[1024,256]{1,0:T(8,128)}), f32[256,256]{1,0:T(8,128)}) %reduce-scatter.13.cloned.1.call-update) | async-done | bytes 262160 | tf_op jit(solution)/shard_map/reduce_scatter | solution.py:82
  367.8 2.4 convert_reduce_fusion.1
  370.4 40.3 %all-gather.6.cloned.1.call-done = bf16[2048,256]{1,0:T(8,128)(2,1)} async-done(((bf16[256,256]{1,0:T(8,128)(2,1)}), bf16[2048,256]{1,0:T(8,128)(2,1)}) %all-gather.6.cloned.1.call-update) | async-done | bytes 1048592 | tf_op jit(solution)/shard_map/all_gather | solution.py:81
  410.8 4.7 fusion.51
  415.6 23.8 %reduce-scatter.15.cloned.1.call-done = f32[256,256]{1,0:T(8,128)} async-done(((f32[1024,256]{1,0:T(8,128)}), f32[256,256]{1,0:T(8,128)}) %reduce-scatter.15.cloned.1.call-update) | async-done | bytes 262160 | tf_op jit(solution)/shard_map/reduce_scatter | solution.py:82
  439.4 2.5 convert_reduce_fusion
  442.0 40.3 %all-gather.8.cloned.1.call-done = bf16[2048,256]{1,0:T(8,128)(2,1)} async-done(((bf16[256,256]{1,0:T(8,128)(2,1)}), bf16[2048,256]{1,0:T(8,128)(2,1)}) %all-gather.8.cloned.1.call-update) | async-done | bytes 1048592 | tf_op jit(solution)/shard_map/all_gather | solution.py:81
  482.2 4.7 fusion.52
  489.5 38.9 %all-reduce = (f32[256,41]{0,1:T(8,128)S(1)}, f32[553]{0:T(1024)S(1)}, f32[]{:T(128)}) all-reduce(f32[256,41]{0,1:T(8,128)} %fusion.36, f32[553]{0:T(1024)S(1)} %pad_maximum_fusion, f32[]{:T(128)} %get-tuple-element.15), channel_id=1, replica_groups=mesh['row'=8,'col'=4] {'row','col'}, use_global_device_ids=true, to_apply=%region_12.14 | all-reduce | flops 11050 | bytes 88400 | tf_op jit(solution)/shard_map/psum | solution.py:124
  534.4 127.7 %all-reduce.4.cloned.1.call-done = (f32[602,256]{1,0:T(8,128)}, f32[256,256]{1,0:T(8,128)}) async-done(((f32[602,256]{1,0:T(8,128)}, f32[256,256]{1,0:T(8,128)}), (f32[602,256]{1,0:T(8,128)}, f32[256,256]{1,0:T(8,128)})) %all-reduce.4.cloned.1.call-update) | async-done | bytes 878608 | tf_op jit(solution)/shard_map/psum | solution.py:124
  662.1 2.7 multiply_subtract_fusion
  (94 shorter events, 22.9 us)
Async XLA Ops:
  7.2 89.7 %reduce-scatter.7.cloned.1.call-start = ((), (), s32[]{:S(2)}) async-start(), calls=%async_computation.6 | async-start | bytes 2359296 | tf_op jit(solution)/shard_map/reduce_scatter | solution.py:73
  25.6 72.4 %copy-start.6 = (f32[256,256]{1,0:T(8,128)S(1)}, f32[256,256]{1,0:T(8,128)}, u32[]{:S(2)}) copy-start(f32[256,256]{1,0:T(8,128)} %param.26) | copy-start | bytes 786436
  28.2 148.0 %reduce-scatter.9.cloned.1.call-start = ((), (), s32[]{:S(2)}) async-start(), calls=%async_computation.7 | async-start | bytes 2359296 | tf_op jit(solution)/shard_map/reduce_scatter | solution.py:73
  110.1 145.3 %reduce-scatter.11.cloned.1.call-start = ((), (), s32[]{:S(2)}) async-start(), calls=%async_computation.8 | async-start | bytes 2359296 | tf_op jit(solution)/shard_map/reduce_scatter | solution.py:73
  184.5 71.0 %copy-start.12 = (f32[256,41]{0,1:T(8,128)S(1)}, f32[256,41]{0,1:T(8,128)}, u32[]{:S(2)}) copy-start(f32[256,41]{0,1:T(8,128)} %param.27) | copy-start | bytes 125956
  184.5 72.2 %copy-start.22 = (s32[256]{0:T(256)S(1)}, s32[256]{0:T(256)}, u32[]{:S(2)}) copy-start(s32[256]{0:T(256)} %param.22) | copy-start | bytes 3076
  184.5 72.2 %copy-start.21 = (s32[256]{0:T(256)S(1)}, s32[256]{0:T(256)}, u32[]{:S(2)}) copy-start(s32[256]{0:T(256)} %param.23) | copy-start | bytes 3076
  189.3 149.9 %all-gather.4.cloned.1.call-start = ((), (), s32[]{:S(2)}) async-start(), calls=%async_computation.9 | async-start | bytes 1179648 | tf_op jit(solution)/shard_map/all_gather | solution.py:81
  299.3 68.5 %copy-start.4 = (bf16[256,256]{1,0:T(8,128)(2,1)S(1)}, bf16[256,256]{1,0:T(8,128)(2,1)}, u32[]{:S(2)}) copy-start(bf16[256,256]{1,0:T(8,128)(2,1)} %convolution_convert_fusion.2) | copy-start | bytes 393220
  299.3 68.5 %copy-start.8 = (f32[256,256]{1,0:T(8,128)S(1)}, f32[256,256]{1,0:T(8,128)}, u32[]{:S(2)}) copy-start(f32[256,256]{1,0:T(8,128)} %reduce-scatter.9.cloned.1.call-done) | copy-start | bytes 786436
  299.3 68.5 %reduce-scatter.13.cloned.1.call-start = ((), (), s32[]{:S(2)}) async-start(), calls=%async_computation.10 | async-start | bytes 1310720 | tf_op jit(solution)/shard_map/reduce_scatter | solution.py:82
  344.0 66.8 %all-gather.6.cloned.1.call-start = ((), (), s32[]{:S(2)}) async-start(), calls=%async_computation.11 | async-start | bytes 1179648 | tf_op jit(solution)/shard_map/all_gather | solution.py:81
  370.2 69.2 %copy-start.5 = (bf16[256,256]{1,0:T(8,128)(2,1)S(1)}, bf16[256,256]{1,0:T(8,128)(2,1)}, u32[]{:S(2)}) copy-start(bf16[256,256]{1,0:T(8,128)(2,1)} %get-tuple-element.29) | copy-start | bytes 393220
  370.2 69.2 %copy-start.16 = (f32[256,256]{1,0:T(8,128)S(1)}, f32[256,256]{1,0:T(8,128)}, u32[]{:S(2)}) copy-start(f32[256,256]{1,0:T(8,128)} %reduce-scatter.7.cloned.1.call-done) | copy-start | bytes 786436
  370.2 69.1 %reduce-scatter.15.cloned.1.call-start = ((), (), s32[]{:S(2)}) async-start(), calls=%async_computation.12 | async-start | bytes 1310720 | tf_op jit(solution)/shard_map/reduce_scatter | solution.py:82
  415.5 66.7 %all-gather.8.cloned.1.call-start = ((), (), s32[]{:S(2)}) async-start(), calls=%async_computation.13 | async-start | bytes 1179648 | tf_op jit(solution)/shard_map/all_gather | solution.py:81
  441.9 88.3 %copy-start.11 = (bf16[256,256]{1,0:T(8,128)(2,1)S(1)}, bf16[256,256]{1,0:T(8,128)(2,1)}, u32[]{:S(2)}) copy-start(bf16[256,256]{1,0:T(8,128)(2,1)} %get-tuple-element.43) | copy-start | bytes 393220
  441.9 88.3 %reduce-scatter.17.cloned.1.call-start = ((), (), s32[]{:S(2)}) async-start(), calls=%async_computation.14 | async-start | bytes 1310720 | tf_op jit(solution)/shard_map/reduce_scatter | solution.py:82
  487.0 45.3 %copy-start.20 = (f32[553]{0:T(1024)S(1)}, f32[553]{0:T(1024)}, u32[]{:S(2)}) copy-start(f32[553]{0:T(1024)} %param.32) | copy-start | bytes 6640
  487.0 175.2 %copy-start.9 = (f32[602,256]{1,0:T(8,128)S(1)}, f32[602,256]{1,0:T(8,128)}, u32[]{:S(2)}) copy-start(f32[602,256]{1,0:T(8,128)} %param.33) | copy-start | bytes 1849348
  487.0 175.2 %copy-start.10 = (f32[602,256]{1,0:T(8,128)S(1)}, f32[602,256]{1,0:T(8,128)}, u32[]{:S(2)}) copy-start(f32[602,256]{1,0:T(8,128)} %param.29) | copy-start | bytes 1849348
  487.0 177.8 %copy-start.13 = (f32[256,256]{1,0:T(8,128)S(1)}, f32[256,256]{1,0:T(8,128)}, u32[]{:S(2)}) copy-start(f32[256,256]{1,0:T(8,128)} %param.34) | copy-start | bytes 786436
  487.0 175.1 %all-reduce.4.cloned.1.call-start = ((), (), s32[]{:S(2)}) async-start(), calls=%async_computation.15 | async-start | bytes 1769472 | tf_op jit(solution)/shard_map/psum | solution.py:124
  488.7 176.1 %copy-start.14 = (f32[256,256]{1,0:T(8,128)S(1)}, f32[256,256]{1,0:T(8,128)}, u32[]{:S(2)}) copy-start(f32[256,256]{1,0:T(8,128)} %param.30) | copy-start | bytes 786436
  (9 other events, 111.1 us)
Sparse Core Ops, SparseCore 0:
  28.3 68.5 reduce-scatter.6
  110.2 65.9 reduce-scatter.8
  189.4 65.9 reduce-scatter.10
  299.4 39.7 all-gather.3
  344.1 23.6 reduce-scatter.12
  370.5 40.1 all-gather.5
  415.7 23.6 reduce-scatter.14
  442.1 40.1 all-gather.7
  487.1 23.6 reduce-scatter.16
  532.4 129.7 all-reduce.3
where the time goes:
time: 673 us
  waiting for transfers between devices  497 us (74%)
  blocking collectives  102 us (15%)
  matrix products  36.9 us (5%)
  other arithmetic  16 us (2%)
  between operations  15.1 us (2%)
    reduce_scatter x3, waiting for transfers between devices, spread(): lax.psum_scatter(jnp.dot(tile, whole, preferred_element_type=jnp.float32)...  201 us
    psum x1, waiting for transfers between devices, shards(): lax.psum((weight_grads[0], weight_grads[1], weight_grads[2], jnp.concaten...  128 us
    all_gather x3, waiting for transfers between devices, collect(): whole = lax.all_gather(grads, 'row', axis=0, tiled=True)  120 us
    reduce_scatter x3, waiting for transfers between devices, collect(): lax.psum_scatter(inner_rows(tile, whole), 'col', scatter_dimension=0, til...  47.5 us
    psum x1, blocking collectives, shards(): total = lax.psum(jnp.sum(counted), ('row', 'col'))  39.8 us
    psum x1, blocking collectives, shards(): lax.psum((weight_grads[0], weight_grads[1], weight_grads[2], jnp.concaten...  38.9 us
    all_gather x3, blocking collectives, spread(): whole = lax.all_gather(values, 'col', axis=0, tiled=True)  23.1 us
    dot_general x6, matrix products, inner_rows(): lax.dot_general(left, right, (((0,), (0,)), ((), ())), preferred_element_...  19.7 us
  transfers between devices with their start and end apart: 10, of which 9 were waited for; matrix products, arithmetic and copies ran while one was open for 1% of the time, Pallas kernels for 0%

commit v1 on v0

v1 whole, which is shorter than its diff:
```python
import functools
import math

import jax
import jax.numpy as jnp
from jax import lax
from jax.experimental import pallas as pl
from jax.experimental.pallas import tpu as pltpu
from jax.sharding import PartitionSpec as P

SUB = 512
STEP = 5


B_ONE = 0.5
B_TWO = 0.5
RATE = 0.05
DECAY = 0.01
EPSILON = 1e-08
SMOOTH = 0.1

MESH = pl.DeviceIdType.MESH
LOW = jnp.bfloat16
FULL = jnp.float32
GELU_A = 0.7978845608028654
GELU_B = 0.044715


def adam_update(weight, first, second, grad):
    first_new = B_ONE * first + (1.0 - B_ONE) * grad
    second_new = B_TWO * second + (1.0 - B_TWO) * grad * grad
    fix_one = 1.0 - B_ONE**STEP
    fix_two = 1.0 - B_TWO**STEP
    step_size = first_new / fix_one / (jnp.sqrt(second_new / fix_two) + EPSILON) + DECAY * weight
    return (first_new, second_new, weight - RATE * step_size)


def up(value, unit):
    return -(-value // unit) * unit


def dot(left, right):
    return jnp.dot(left, right, preferred_element_type=FULL)


def dot_nt(left, right):
    return lax.dot_general(left, right, (((1,), (1,)), ((), ())), preferred_element_type=FULL)


def gelu_both(z):
    t = jnp.tanh(GELU_A * (z + GELU_B * z * z * z))
    half = 0.5 * (1.0 + t)
    slope = half + 0.5 * z * (1.0 - t * t) * (GELU_A * (1.0 + 3.0 * GELU_B * z * z))
    return z * half, slope


class Sizes:
    def __init__(self, n_row, n_col, own, feat, width, classes):
        self.n_row, self.n_col = n_row, n_col
        self.nk = 2 if n_col % 2 == 0 else 1
        self.ny = n_col // self.nk
        self.nx = self.ny if n_row % self.ny == 0 else 1
        self.nz = n_row // self.nx
        self.own, self.feat, self.width, self.classes = own, feat, width, classes
        self.feat_up = up(feat, 128)
        self.cls = up(classes, 16)
        self.plane = self.nx * self.ny
        self.one_rows = up(feat, 16 * self.plane)
        self.two_rows = up(width + self.cls, 16 * self.plane)
        self.grad_rows = self.one_rows + self.two_rows
        self.lanes = width // self.nk
        self.sends = 4 * (n_row + n_col) + 4 * self.plane
        self.arrivals = 6 * n_row + 8 * n_col + 8 * self.plane + 16


def kernel(
    s,
    xt_ref,
    adj_ref,
    occ_ref,
    lab_ref,
    mask_ref,
    cnt_ref,
    w1_ref,
    w2_ref,
    w3t_ref,
    bias_ref,
    grad_ref,
    misc_ref,
    tile,
    w1b,
    w3t,
    xt_all,
    v_all,
    pool,
    xsend,
    zsend,
    zrecv,
    v3_all,
    p3send,
    p3recv,
    dl_all,
    q3send,
    q3recv,
    acc,
    half_send,
    half_recv,
    half,
    plane_recv,
    quarter,
    fin,
    misc_k,
    misc_p,
    misc_z,
    ssem,
    rsem,
    lsem,
):
    nx, ny, nz, nk = s.nx, s.ny, s.nz, s.nk
    own, width = s.own, s.width
    r, c = lax.axis_index("row"), lax.axis_index("col")
    z, x = r // nx, r % nx
    y, k = c // nk, c % nk

    def at(zz, xx, yy, kk):
        return (zz * nx + xx, yy * nk + kk)

    def xs(d):
        return lax.rem(x + d, nx)

    def ys(d):
        return lax.rem(y + d, ny)

    def zs(d):
        if nz & (nz - 1):
            return lax.rem(z + d, nz)
        there, bit = z, 1
        while bit < nz:
            if d & bit:
                there = there + bit - 2 * bit * lax.rem(there // bit, 2)
            bit *= 2
        return there

    def zback(d):
        return zs(d) if not nz & (nz - 1) else lax.rem(z + nz - d, nz)

    sibling = at(z, x, y, 1 - k)

    rows, cols = tile.shape
    n_sub = rows // SUB
    loads = [
        pltpu.make_async_copy(
            adj_ref.at[pl.ds(a * SUB, SUB)], tile.at[pl.ds(a * SUB, SUB)], lsem.at[a]
        )
        for a in range(n_sub)
    ]
    for load in loads:
        load.start()

    peers = []
    for d in range(1, s.n_row):
        peers.append((lax.rem(r + d, s.n_row), c))
    for d in range(1, s.n_col):
        peers.append((r, lax.rem(c + d, s.n_col)))
    for dx in range(1, nx):
        for dy in range(1, ny):
            peers.append(at(z, xs(dx), ys(dy), k))
    barrier = pltpu.get_barrier_semaphore()
    for peer in peers:
        pl.semaphore_signal(barrier, inc=1, device_id=peer, device_id_type=MESH)

    free = list(range(s.sends))
    pending = []

    def send(src, dst, recv_slot, device, of=None):
        if not free:
            settle(len(pending) - 1)
        copy = pltpu.make_async_remote_copy(
            src_ref=src,
            dst_ref=dst,
            send_sem=ssem.at[free[0]],
            recv_sem=rsem.at[recv_slot],
            device_id=device,
            device_id_type=MESH,
        )
        copy.start()
        pending.append((copy, free.pop(0), of))

    def arrived(dst, recv_slot):
        pltpu.make_async_remote_copy(
            src_ref=dst,
            dst_ref=dst,
            send_sem=ssem.at[0],
            recv_sem=rsem.at[recv_slot],
            device_id=sibling,
            device_id_type=MESH,
        ).wait_recv()

    def settle(keep=0, of=None):
        done = [p for p in pending if p[2] == of] if of else pending[: len(pending) - keep]
        for item in done:
            item[0].wait_send()
            free.append(item[1])
        left = [p for p in pending if all(p is not q for q in done)]
        pending[:] = left

    rcount = [0]

    def rslots(n):
        rcount[0] += n
        return rcount[0] - n

    def row_block(index):
        return pl.ds(pl.multiple_of(index * own, own), own)

    nh = 2
    cut = own // nh

    def row_part(index, q):
        return pl.ds(pl.multiple_of(index * own + q * cut, cut), cut)

    def part(q):
        return pl.ds(q * cut, cut)

    valid_col = (lax.broadcasted_iota(jnp.int32, (own, width), 0) < cnt_ref[0]).astype(FULL)
    valid_low = valid_col.astype(LOW)
    valid_row = (lax.broadcasted_iota(jnp.int32, (1, own), 1) < cnt_ref[0]).astype(FULL)
    counted = mask_ref[...].astype(FULL) * valid_row

    pad = s.feat_up - up(s.feat, 16) + 16
    own_xt = xt_all.at[c]
    own_xt[s.feat_up - pad :, :] = jnp.zeros((pad, own), LOW)
    w1b[s.feat_up - pad :, :] = jnp.zeros((pad, width), LOW)
    x_valid = (lax.broadcasted_iota(jnp.int32, (s.feat, own), 1) < cnt_ref[0]).astype(LOW)
    own_xt[: s.feat, :] = xt_ref[...] * x_valid
    w1b[: s.feat, :] = w1_ref[...].astype(LOW)
    y1 = lax.dot_general(
        own_xt[...], w1b[...], (((0,), (0,)), ((), ())), preferred_element_type=FULL
    ).astype(LOW)

    wide = [rslots(s.n_row * nh) for _ in range(2)]
    gbase = [rslots(s.n_col * nh) for _ in range(2)]

    def start_gather(hop, q, values):
        mine = v_all.at[hop, row_part(c, q)]
        mine[...] = values
        for d in range(1, ny):
            send(mine, mine, gbase[hop] + c * nh + q, at(z, x, ys(d), k))
        if nk > 1:
            send(mine, mine, gbase[hop] + c * nh + q, sibling)

    def complete_gather(hop):
        for q in range(nh):
            for d in range(1, ny):
                source = ys(ny - d) * nk + k
                block = v_all.at[hop, row_part(source, q)]
                arrived(block, gbase[hop] + source * nh + q)
                if nk > 1:
                    send(block, block, gbase[hop] + source * nh + q, sibling)
        if nk > 1:
            for q in range(nh):
                for d in range(ny):
                    source = ys(d) * nk + 1 - k
                    arrived(
                        v_all.at[hop, row_part(source, q)], gbase[hop] + source * nh + q
                    )

    pl.semaphore_wait(barrier, len(peers))
    for q in range(nh):
        start_gather(0, q, y1[q * cut : (q + 1) * cut])

    w3t[...] = jnp.zeros_like(w3t)
    w3t[: s.classes, :] = w3t_ref[...].astype(LOW)
    w2 = w2_ref[...].astype(LOW)
    for a in range(n_sub):
        loads[a].wait()
        for b in range(cols // own):
            piece = tile[pl.ds(a * SUB, SUB), pl.ds(b * own, own)]
            cover = jnp.full((SUB, own), occ_ref[a, b].astype(FULL), FULL).astype(LOW)
            tile[pl.ds(a * SUB, SUB), pl.ds(b * own, own)] = piece * cover

    def spread(hop, finish):
        settle(of="hop")
        with jax.named_scope("gather_y"):
            complete_gather(hop)
        zbase = wide[hop]
        xbase = zbase + nz * nh
        order = list(range(nz - 1, -1, -1))

        def send_x(dz, dx, q):
            place = (dx - 1) * nz + dz
            send(
                xsend.at[place, part(q)],
                pool.at[hop * s.n_row + place, part(q)],
                xbase + place * nh + q,
                at(z, xs(dx), y, k),
                "hop",
            )

        with jax.named_scope("send_x"):
            for dz in order:
                for dx in range(1, nx):
                    place = (dx - 1) * nz + dz
                    rt = zs(dz) * nx + xs(dx)
                    xsend[place] = dot(tile[row_block(rt), :], v_all[hop]).astype(LOW)
                    send_x(dz, dx, 0)
            for q in range(1, nh):
                for dz in order:
                    for dx in range(1, nx):
                        send_x(dz, dx, q)
            for dz in order:
                acc[:, dz * own : (dz + 1) * own] = dot(
                    tile[row_block(zs(dz) * nx + x), :], v_all[hop]
                )

        def send_z(dz, q):
            rows_q = slice(q * cut, (q + 1) * cut)
            total = acc[rows_q, dz * own : (dz + 1) * own]
            for dx in range(1, nx):
                place = (dx - 1) * nz + dz
                arrived(pool.at[hop * s.n_row + place, part(q)], xbase + place * nh + q)
                total = total + pool[hop * s.n_row + place, rows_q, :].astype(FULL)
            if dz:
                zsend[dz - 1, rows_q, :] = total.astype(LOW)
                send(
                    zsend.at[dz - 1, part(q)],
                    zrecv.at[hop, dz - 1, part(q)],
                    zbase + dz * nh + q,
                    at(zs(dz), x, y, k),
                    "hop",
                )
            return total

        totals = [None] * nh

        def sum_z(q):
            total = totals[q]
            rows_q = slice(q * cut, (q + 1) * cut)
            for dz in range(1, nz):
                arrived(zrecv.at[hop, dz - 1, part(q)], zbase + dz * nh + q)
                total = total + zrecv[hop, dz - 1, rows_q, :].astype(FULL)
            finish(q, total)

        with jax.named_scope("send_z"):
            for q in range(nh):
                for i, dz in enumerate(order):
                    totals[q] = send_z(dz, q)
                    if q and i == nz // 2 - 1:
                        with jax.named_scope("sum_z0"):
                            sum_z(q - 1)
        with jax.named_scope("sum_z1"):
            sum_z(nh - 1)

    bias = [bias_ref[i * width : (i + 1) * width].reshape(1, width) for i in range(2)]
    slopes, acts = [None] * nh, [None] * nh

    def first_done(q, total):
        rows_q = slice(q * cut, (q + 1) * cut)
        z1 = total + v_all[0, row_part(c, q), :].astype(FULL) + bias[0]
        act, slope = gelu_both(z1)
        h1 = act.astype(LOW) * valid_low[rows_q]
        start_gather(1, q, dot(h1, w2).astype(LOW))
        acts[q], slopes[q] = h1, slope * valid_col[rows_q]

    spread(0, first_done)
    h1t = jnp.concatenate(acts, axis=0).astype(FULL).T.astype(LOW)
    slope1t = jnp.concatenate(slopes, axis=0).T

    xt_base = rslots(s.n_col)

    def second_done(q, total):
        rows_q = slice(q * cut, (q + 1) * cut)
        z2 = total + v_all[1, row_part(c, q), :].astype(FULL) + bias[1]
        act, slope = gelu_both(z2)
        acts[q] = act.astype(LOW) * valid_low[rows_q]
        slopes[q] = slope * valid_col[rows_q]

    spread(1, second_done)
    h2 = jnp.concatenate(acts, axis=0)
    y3t = dot_nt(w3t[...], h2).astype(LOW)

    with jax.named_scope("hop3_gather"):
        base = rslots(s.n_col)
        mine = v3_all.at[c]
        mine[...] = y3t
        for d in range(1, s.n_col):
            send(mine, mine, base + c, (r, lax.rem(c + d, s.n_col)))
        slope2t = jnp.concatenate(slopes, axis=0).T
        settle(s.n_col - 1)
        for d in range(1, s.n_col):
            source = lax.rem(c + d, s.n_col)
            arrived(v3_all.at[source], base + source)
    with jax.named_scope("hop3_sum"):
        pbase = rslots(s.n_row)
        v3 = jnp.concatenate([v3_all[i] for i in range(s.n_col)], axis=1)
        for d in range(s.n_row - 1, -1, -1):
            rt = lax.rem(r + d, s.n_row)
            here = dot_nt(v3, tile[row_block(rt), :])
            if d:
                p3send[d - 1] = here.astype(LOW)
                send(p3send.at[d - 1], p3recv.at[d - 1], pbase + d, (rt, c))
            else:
                total = here
        for d in range(1, s.n_row):
            arrived(p3recv.at[d - 1], pbase + d)
            total = total + p3recv[d - 1].astype(FULL)
    total = total + y3t.astype(FULL)

    place = lax.broadcasted_iota(jnp.int32, (s.cls, own), 0)
    real = place < s.classes
    on_diag = lax.broadcasted_iota(jnp.int32, (s.cls, s.classes), 0) == lax.broadcasted_iota(
        jnp.int32, (s.cls, s.classes), 1
    )
    bias3 = jnp.sum(
        jnp.where(on_diag, bias_ref[2 * width :].reshape(1, s.classes), 0.0), axis=1, keepdims=True
    )
    logits = jnp.where(real, total + bias3, -1e30)
    shifted = logits - jnp.max(logits, axis=0, keepdims=True)
    weight = jnp.where(real, jnp.exp(shifted), 0.0)
    norm = jnp.sum(weight, axis=0, keepdims=True)
    logp = shifted - jnp.log(norm)
    target = jnp.where(place == lab_ref[...], 1.0 - SMOOTH, 0.0) + SMOOTH / s.classes
    target = jnp.where(real, target, 0.0)
    row_loss = -jnp.sum(jnp.where(real, target * logp, 0.0), axis=0, keepdims=True)
    loss = jnp.sum(row_loss * counted, axis=1, keepdims=True)
    number = jnp.sum(counted, axis=1, keepdims=True)
    dlt = ((weight / norm - target) * counted).astype(LOW)

    with jax.named_scope("back3_gather"):
        base = rslots(s.n_row)
        mine = dl_all.at[r]
        mine[...] = dlt
        for d in range(s.n_row - 1, 0, -1):
            send(mine, mine, base + r, (lax.rem(r + d, s.n_row), c))
        here = dot(dlt, tile[row_block(r), :])
        for d in range(1, s.n_row):
            source = lax.rem(r + d, s.n_row)
            arrived(dl_all.at[source], base + source)
            here = here + dot(dl_all[source], tile[row_block(source), :])
        acc[: s.cls, :cols] = here
    with jax.named_scope("back3_sum"):
        qbase = rslots(s.n_col)
        total = dlt.astype(FULL)
        for d in range(s.n_col - 1, -1, -1):
            ct = lax.rem(c + d, s.n_col)
            here = acc[: s.cls, row_block(ct)]
            if d:
                q3send[d - 1] = here.astype(LOW)
                send(q3send.at[d - 1], q3recv.at[d - 1], qbase + d, (r, ct))
            else:
                total = total + here
        for d in range(1, s.n_col):
            arrived(q3recv.at[d - 1], qbase + d)
            total = total + q3recv[d - 1].astype(FULL)
    qt = total.astype(LOW)
    dh2t = lax.dot_general(
        w3t[...], qt, (((0,), (0,)), ((), ())), preferred_element_type=FULL
    )
    step_cols = min(cols, 1024)

    def gained(values, block, fresh=False):
        for j in range(0, cols, step_cols):
            here = dot(values, tile[block, j : j + step_cols])
            if fresh:
                acc[:, j : j + step_cols] = here
            else:
                acc[:, j : j + step_cols] += here

    def receive(hop, values, meanwhile=None):
        base = wide[hop]
        first = hop * s.n_row
        pool[first] = values
        for q in range(nh):
            mine = pool.at[first, part(q)]
            for dz in range(nz - 1, 0, -1):
                send(
                    mine,
                    pool.at[first + dz, part(q)],
                    base + dz * nh + q,
                    at(zs(dz), x, y, k),
                )
            for dx in range(1, nx):
                place = dx * nz
                send(
                    mine,
                    pool.at[first + place, part(q)],
                    base + place * nh + q,
                    at(z, xs(dx), y, k),
                )

        def source(dz, dx):
            return row_block(zback(dz) * nx + xs(nx - dx))

        gained(values, row_block(r), fresh=True)
        if meanwhile is not None:
            meanwhile()
        for q in range(nh):
            for dz in range(1, nz):
                arrived(pool.at[first + dz, part(q)], base + dz * nh + q)
                for dx in range(1, nx):
                    place = dx * nz + dz
                    send(
                        pool.at[first + dz, part(q)],
                        pool.at[first + place, part(q)],
                        base + place * nh + q,
                        at(z, xs(dx), y, k),
                    )
                if q == nh - 1:
                    gained(pool[first + dz], source(dz, 0))
        for dz in range(nz):
            for dx in range(1, nx):
                place = dx * nz + dz
                for q in range(nh):
                    arrived(pool.at[first + place, part(q)], base + place * nh + q)
                gained(pool[first + place], source(dz, dx))

    dz2t = (dh2t * slope2t).astype(LOW)

    def features_out():
        for d in range(1, ny):
            send(own_xt, own_xt, xt_base + c, at(z, x, ys(d), k))
        if nk > 1:
            send(own_xt, own_xt, xt_base + c, sibling)

    with jax.named_scope("back2_rows"):
        settle()
        receive(0, dz2t, features_out)
    with jax.named_scope("back2_cols"):
        cbase = rslots(ny)
        ybase = rslots(ny)

        def crecv(dy):
            return v_all.at[0, dy * own : (dy + 1) * own]

        def yrecv(dy):
            return crecv(dy + (ny if nk > 1 else 0))

        for dy in range(ny - 1, -1, -1):
            if nk > 1:
                xsend[dy] = acc[:, row_block(ys(dy) * nk + 1 - k)].astype(LOW)
                send(xsend.at[dy], crecv(dy), cbase + dy, sibling)
        total = dz2t.astype(FULL)
        for dy in range(ny - 1, -1, -1):
            here = acc[:, row_block(ys(dy) * nk + k)]
            if nk > 1:
                arrived(crecv(dy), cbase + dy)
                here = here + crecv(dy)[...].astype(FULL)
            if dy:
                xsend[ny + dy] = here.astype(LOW)
                send(xsend.at[ny + dy], yrecv(dy), ybase + dy, at(z, x, ys(dy), k))
            else:
                total = total + here
        for d in range(1, ny):
            source = ys(ny - d) * nk + k
            arrived(xt_all.at[source], xt_base + source)
            if nk > 1:
                send(xt_all.at[source], xt_all.at[source], xt_base + source, sibling)
        for dy in range(1, ny):
            arrived(yrecv(dy), ybase + dy)
            total = total + yrecv(dy)[...].astype(FULL)
    dy2t = total.astype(LOW)
    dz1t = (dot(w2, dy2t) * slope1t).astype(LOW)

    lanes, plane = s.lanes, s.plane
    me = y * nx + x
    others = [(dx, dy) for dx in range(nx) for dy in range(ny) if dx or dy]

    def lane_block(index):
        return pl.ds(pl.multiple_of(index * lanes, lanes), lanes)

    class Total:
        def __init__(self, start, rows):
            self.all = pl.ds(start, rows)
            self.start, self.rows = start, rows
            self.n = rows // plane
            self.short = pl.ds(start // plane, self.n)
            self.base = rslots(1 + 3 * plane + nz)

        def piece(self, index):
            return pl.ds(pl.multiple_of(self.start + index * self.n, 16), self.n)

        def core_send(self, other):
            if nk > 1:
                half_send[self.all, :] = other.astype(LOW)
                send(half_send.at[self.all], half_recv.at[self.all], self.base, sibling)

        def plane_send(self, mine):
            if nk > 1:
                arrived(half_recv.at[self.all], self.base)
                mine = mine + half_recv[self.all, :].astype(FULL)
            half[self.all, :] = mine.astype(LOW)
            base = self.base + 1
            for dx, dy in others:
                there = ys(dy) * nx + xs(dx)
                send(
                    half.at[self.piece(there)],
                    plane_recv.at[me, self.short],
                    base + me,
                    at(z, xs(dx), ys(dy), k),
                )
            plane_recv[me, self.short, :] = half[self.piece(me), :]

        def line_send(self):
            base = self.base + 1
            for dx, dy in others:
                there = ys(dy) * nx + xs(dx)
                arrived(plane_recv.at[there, self.short], base + there)
            total = plane_recv[0, self.short, :].astype(FULL)
            for i in range(1, plane):
                total = total + plane_recv[i, self.short, :].astype(FULL)
            quarter[z, self.short, :] = total.astype(LOW)
            mine = quarter.at[z, self.short]
            base = self.base + 1 + plane
            for dz in range(nz - 1, 0, -1):
                send(mine, mine, base + z, at(zs(dz), x, y, k))

        def back_send(self):
            base = self.base + 1 + plane
            for dz in range(1, nz):
                arrived(quarter.at[zback(dz), self.short], base + zback(dz))
            total = quarter[0, self.short, :].astype(FULL)
            for i in range(1, nz):
                total = total + quarter[i, self.short, :].astype(FULL)
            base = self.base + 1 + plane + nz
            mine = fin.at[k, self.piece(me)]
            mine[...] = total.astype(LOW)
            for dx, dy in others:
                send(mine, mine, base + me, at(z, xs(dx), ys(dy), k))
            if nk > 1:
                send(mine, mine, base + plane + me, sibling)

        def back_forward(self):
            base = self.base + 1 + plane + nz
            for dx, dy in others:
                there = ys(dy) * nx + xs(dx)
                block = fin.at[k, self.piece(there)]
                arrived(block, base + there)
                if nk > 1:
                    send(block, block, base + plane + there, sibling)

        def end(self):
            base = self.base + 1 + plane + nz
            if nk > 1:
                for i in range(plane):
                    arrived(fin.at[1 - k, self.piece(i)], base + plane + i)

    one = Total(0, s.one_rows)
    two = Total(s.one_rows, s.two_rows)
    tail = s.two_rows - width - s.cls

    def early():
        grad3t = dot(qt, h2)
        grad2 = dot_nt(h1t, dy2t)
        acc_two = jnp.concatenate(
            [grad2, grad3t] + ([jnp.zeros((tail, width), FULL)] if tail else []), axis=0
        )
        if nk > 1:
            first, second = acc_two[:, :lanes], acc_two[:, lanes:]
            low_core = (k == 0).astype(FULL)
            two.core_send(second * low_core + first * (1.0 - low_core))
            two.plane_send(first * low_core + second * (1.0 - low_core))
        else:
            two.plane_send(acc_two)

    with jax.named_scope("back1_rows"):
        receive(1, dz1t, early)
    with jax.named_scope("grad1"):
        two.line_send()
        acc[:, row_block(c)] += dz1t.astype(FULL)
        if nk > 1:
            for d in range(ny):
                source = ys(d) * nk + 1 - k
                arrived(xt_all.at[source], xt_base + source)

        def grad_one(index):
            total = None
            for i in range(s.n_col):
                here = acc[pl.ds(pl.multiple_of(index * lanes, lanes), lanes), :]
                here = dot_nt(xt_all[i], here[:, i * own : (i + 1) * own].astype(LOW))
                total = here if total is None else total + here
            if s.one_rows <= s.feat_up:
                return total[: s.one_rows]
            return jnp.concatenate(
                [total, jnp.zeros((s.one_rows - s.feat_up, lanes), FULL)], axis=0
            )

        if nk > 1:
            one.core_send(grad_one(1 - k))
        mine_one = grad_one(k)
        ones = jnp.ones((8, own), LOW)
        line = lax.broadcasted_iota(jnp.int32, (8, width), 0)
        lane = lax.broadcasted_iota(jnp.int32, (8, width), 1)
        bias_three = jnp.concatenate([dlt, jnp.zeros((width - s.cls, own), LOW)], axis=0)
        misc = jnp.where(line == 0, dot_nt(ones, dz1t), 0.0)
        misc = jnp.where(line == 1, dot_nt(ones, dz2t), misc)
        misc = jnp.where(line == 2, dot_nt(ones, bias_three), misc)
        misc = jnp.where((line == 3) & (lane == 0), loss, misc)
        misc = jnp.where((line == 3) & (lane == 1), number, misc)
        mbase = rslots(1 + plane + nz)
        misc_k[0] = misc
        if nk > 1:
            send(misc_k.at[0], misc_k.at[1], mbase, sibling)

    with jax.named_scope("sum_plane"):
        one.plane_send(mine_one)
        if nk > 1:
            arrived(misc_k.at[1], mbase)
            misc = misc_k[0] + misc_k[1]
        misc_p[me] = misc
        mbase = mbase + 1
        for dx, dy in others:
            send(misc_p.at[me], misc_p.at[me], mbase + me, at(z, xs(dx), ys(dy), k))
        left = len(pending)
        two.back_send()
    with jax.named_scope("sum_line"):
        one.line_send()
        for dx, dy in others:
            there = ys(dy) * nx + xs(dx)
            arrived(misc_p.at[there], mbase + there)
        misc = misc_p[0]
        for i in range(1, plane):
            misc = misc + misc_p[i]
        mbase = mbase + plane
        misc_z[z] = misc
        for dz in range(1, nz):
            send(misc_z.at[z], misc_z.at[z], mbase + z, at(zs(dz), x, y, k))
        two.back_forward()
        two.end()
        settle(len(pending) - left)
    with jax.named_scope("back_line"):
        one.back_send()
        for dz in range(1, nz):
            arrived(misc_z.at[zback(dz)], mbase + zback(dz))
        misc = misc_z[0]
        for i in range(1, nz):
            misc = misc + misc_z[i]
        misc_ref[...] = jnp.where(line == 4, 1.0 / misc[3:4, 1:2], misc)
        grad_ref[:, s.one_rows :, :] = fin[:, s.one_rows :, :]
    with jax.named_scope("back_plane"):
        one.back_forward()
        one.end()
        grad_ref[:, : s.one_rows, :] = fin[:, : s.one_rows, :]
    with jax.named_scope("settle"):
        settle()
    assert rcount[0] <= s.arrivals


def adam_kernel(
    s, grad_ref, misc_ref, *refs
):
    ins, outs = refs[:12], refs[12:]
    width, classes, f = s.width, s.classes, s.one_rows
    total = misc_ref[3:4, 1:2]
    scale = misc_ref[4:5, 0:1]
    lanes = s.lanes

    def update(place, rows, lane, grad):
        weight, first, second = (ins[3 * place + i][rows, lane] for i in range(3))
        new = adam_update(weight, first, second, grad * scale)
        for i in range(3):
            outs[3 * place + i][rows, lane] = new[i]

    for i in range(s.nk):
        lane = slice(i * lanes, (i + 1) * lanes)
        update(0, slice(0, s.feat), lane, grad_ref[i, : s.feat, :].astype(FULL))
        update(1, slice(0, width), lane, grad_ref[i, f : f + width, :].astype(FULL))
        update(
            2,
            slice(0, classes),
            lane,
            grad_ref[i, f + width : f + width + s.cls, :].astype(FULL)[:classes],
        )
    for i, size in enumerate((width, width, classes)):
        span = slice(i * width, i * width + size)
        weight, first, second = (ins[9 + j][span] for j in range(3))
        new = adam_update(weight, first, second, misc_ref[i, :size] * misc_ref[4, :size])
        for j in range(3):
            outs[9 + j][span] = new[j]
    outs[12][...] = misc_ref[3:4, 0:1]
    outs[13][...] = total


def shards(
    sizes,
    features,
    adjacency,
    occupancy,
    labels,
    train_mask,
    node_count,
    weight_one,
    weight_two,
    weight_three,
    biases,
    first_one,
    first_two,
    first_three,
    first_bias,
    second_one,
    second_two,
    second_three,
    second_bias,
):
    own, feat = features.shape
    width = weight_two.shape[0]
    classes = weight_three.shape[1]
    s = sizes(own, feat, width, classes)
    rows, cols = adjacency.shape
    lanes = s.lanes
    vmem = pl.BlockSpec(memory_space=pltpu.VMEM)
    smem = pl.BlockSpec(memory_space=pltpu.SMEM)
    block = (own, width)
    small = (s.cls, own)
    shapes = [
        ((rows, cols), LOW),
        ((s.feat_up, width), LOW),
        ((s.cls, width), LOW),
        ((s.n_col, s.feat_up, own), LOW),
        ((2, s.n_col * own, width), LOW),
        ((2 * s.n_row, *block), LOW),
        ((max(2 * s.ny, s.n_row - s.nz), *block), LOW),
        ((max(1, s.nz - 1), *block), LOW),
        ((2, max(1, s.nz - 1), *block), LOW),
        ((s.n_col, *small), LOW),
        ((s.n_row, *small), LOW),
        ((s.n_row, *small), LOW),
        ((s.n_row, *small), LOW),
        ((s.n_col, *small), LOW),
        ((s.n_col, *small), LOW),
        ((width, max(cols, s.nz * own)), FULL),
        ((s.grad_rows, lanes), LOW),
        ((s.grad_rows, lanes), LOW),
        ((s.grad_rows, lanes), LOW),
        ((s.plane, s.grad_rows // s.plane, lanes), LOW),
        ((s.nz, s.grad_rows // s.plane, lanes), LOW),
        ((s.nk, s.grad_rows, lanes), LOW),
        ((2, 8, width), FULL),
        ((s.plane, 8, width), FULL),
        ((s.nz, 8, width), FULL),
    ]
    bytes_held = sum(math.prod(shape) * jnp.dtype(kind).itemsize for shape, kind in shapes)
    limit = 62 * 2**20
    grads, misc = pl.pallas_call(
        functools.partial(kernel, s),
        out_shape=(
            jax.ShapeDtypeStruct((s.nk, s.grad_rows, lanes), LOW),
            jax.ShapeDtypeStruct((8, width), FULL),
        ),
        in_specs=[
            vmem,
            pl.BlockSpec(memory_space=pl.ANY),
            smem,
            vmem,
            vmem,
            smem,
            vmem,
            vmem,
            vmem,
            vmem,
        ],
        out_specs=(vmem, vmem),
        scratch_shapes=[
            *[pltpu.VMEM(shape, kind) for shape, kind in shapes],
            pltpu.SemaphoreType.DMA((s.sends,)),
            pltpu.SemaphoreType.DMA((s.arrivals,)),
            pltpu.SemaphoreType.DMA((rows // SUB,)),
        ],
        compiler_params=pltpu.CompilerParams(
            collective_id=0, has_side_effects=True, vmem_limit_bytes=limit
        ),
        cost_estimate=pl.CostEstimate(
            flops=12 * rows * cols * width, bytes_accessed=2 * rows * cols, transcendentals=0
        ),
        name="step",
    )(
        features.T,
        adjacency,
        occupancy,
        labels.reshape(1, own),
        train_mask.reshape(1, own),
        node_count,
        weight_one,
        weight_two,
        weight_three.T,
        biases,
    )
    state = (
        weight_one,
        first_one,
        second_one,
        weight_two,
        first_two,
        second_two,
        weight_three.T,
        first_three.T,
        second_three.T,
        biases,
        first_bias,
        second_bias,
    )
    new = pl.pallas_call(
        functools.partial(adam_kernel, s),
        out_shape=(
            *[jax.ShapeDtypeStruct(a.shape, FULL) for a in state],
            jax.ShapeDtypeStruct((1, 1), FULL),
            jax.ShapeDtypeStruct((1, 1), FULL),
        ),
        in_specs=[vmem] * 14,
        out_specs=(vmem,) * 14,
        compiler_params=pltpu.CompilerParams(vmem_limit_bytes=62 * 2**20),
        name="update",
    )(grads, misc, *state)
    return (
        *new[:6],
        *[a.T for a in new[6:9]],
        *new[9:12],
        new[12].reshape(()),
        new[13].reshape(()),
    )


def solution(mesh):
    placed = (
        P(("row", "col"), None),
        P("col", "row"),
        P("col", "row"),
        P(("row", "col")),
        P(("row", "col")),
        P(("row", "col")),
        *[P()] * 12,
    )
    sizes = functools.partial(Sizes, mesh.shape["row"], mesh.shape["col"])
    return jax.shard_map(
        functools.partial(shards, sizes),
        mesh=mesh,
        in_specs=placed,
        out_specs=(P(),) * 14,
        check_vma=False,
    )
```

time: 673 us -> 137 us (0.20)
  waiting for transfers between devices: 497 us -> 0 us
  Pallas kernels: 0 us -> 136 us
  blocking collectives: 102 us -> 0 us
  matrix products: 36.9 us -> 0 us
  other arithmetic: 16 us -> 0 us
  between operations: 15.1 us -> 1.3 us
    reduce_scatter x6 -> x0, waiting for transfers between devices: 248 us -> none  [the longest x3 201 us: spread(): lax.psum_scatter(jnp.dot(tile, whole, preferred_element_type=jnp.float32)...]
    pallas_call x0 -> x2, Pallas kernels: none -> 136 us  [the longest x1 132 us: shards(): pl.pallas_call(functools.partial(kernel, s), out_shape=(jax.ShapeDtypeStr...]
    psum x1 -> x0, waiting for transfers between devices: 128 us -> none  [shards(): lax.psum((weight_grads[0], weight_grads[1], weight_grads[2], jnp.concaten...]
    all_gather x3 -> x0, waiting for transfers between devices: 120 us -> none  [collect(): whole = lax.all_gather(grads, 'row', axis=0, tiled=True)]
    psum x2 -> x0, blocking collectives: 78.6 us -> none  [the longest x1 39.8 us: shards(): total = lax.psum(jnp.sum(counted), ('row', 'col'))]
    dot_general x14 -> x0, matrix products: 36.9 us -> none  [the longest x6 19.7 us: inner_rows(): lax.dot_general(left, right, (((0,), (0,)), ((), ())), preferred_element_...]
    all_gather x3 -> x0, blocking collectives: 23.1 us -> none  [spread(): whole = lax.all_gather(values, 'col', axis=0, tiled=True)]
  transfers between devices with their start and end apart: 10 -> 0, of which waited for: 9 -> 0; matrix products, arithmetic and copies ran while one was open for 1% -> 0% of each run, Pallas kernels for 0% -> 0%
where the time goes in v1:
time: 137 us
  Pallas kernels  136 us (99%)
    pallas_call x1, Pallas kernels, shards(): pl.pallas_call(functools.partial(kernel, s), out_shape=(jax.ShapeDtypeStr...  132 us
    pallas_call x1, Pallas kernels, shards(): pl.pallas_call(functools.partial(adam_kernel, s), out_shape=(*[jax.ShapeD...  4.16 us

profile of v1, /device:TPU:0, one launch (start us, length us, event | category | flops | bytes accessed | tf_op | source)
XLA Modules:
  0.0 137.0 jit_solution(13759075534230969191)
XLA Ops:
  1.3 131.6 %step.1 = (bf16[2,960,128]{2,1,0:T(8,128)(2,1)}, f32[8,256]{1,0:T(8,128)}) custom-call(bf16[602,256]{1,0:T(8,128)(2,1)} %bitcast.15, bf16[2048,1024]{1,0:T(8,128)(2,1)} %adj_ref.1, s32[4,4]{1,0:T(4,128)} %occ_ref.1, s32[1,256]{1,0:T(1,128)} %bitcast.19, s32[1,256]{1,0:T(1,128)} %bitcast.20, s32[1]{0:T(128)S(6)} %copy.32.cnt_ref, f32[602,256]{1,0:T(8,128)} %refs_0_.1, ...), custom_call_target="tpu_custom_call" | custom-call | flops 6442450944 | bytes 4194304 | tf_op jit(solution)/shard_map/step/pallas_call | solution.py:843
  132.9 4.2 %update.1 = (f32[602,256]{1,0:T(8,128)}, f32[602,256]{1,0:T(8,128)}, f32[602,256]{1,0:T(8,128)}, f32[256,256]{1,0:T(8,128)}, f32[256,256]{1,0:T(8,128)}, /*index...) custom-call(bf16[2,960,128]{2,1,0:T(8,128)(2,1)} %get-tuple-element., ...), custom_call_target="tpu_custom_call" | custom-call | tf_op jit(solution)/shard_map/update/pallas_call | solution.py:901

commit v2 on v1

--- a/solution.py
+++ b/solution.py
@@ -69,8 +69,13 @@
         self.two_rows = up(width + self.cls, 16 * self.plane)
         self.grad_rows = self.one_rows + self.two_rows
         self.lanes = width // self.nk
-        self.sends = 4 * (n_row + n_col) + 4 * self.plane
-        self.arrivals = 6 * n_row + 8 * n_col + 8 * self.plane + 16
+        units = self.one_rows // (16 * self.plane)
+        self.cut_rows = (units + 1) // 2 * 16 * self.plane
+        self.nh = 4
+        self.sends = 3 * (n_row + n_col) + 3 * self.plane
+        wide = 2 * self.nh * (n_row + n_col)
+        self.arrivals = wide + 2 * (n_row + n_col) + n_col + 4 * self.ny
+        self.arrivals += 3 * (1 + 3 * self.plane + self.nz) + 1 + self.plane + self.nz
 
 
 def kernel(
@@ -172,7 +177,7 @@
     free = list(range(s.sends))
     pending = []
 
-    def send(src, dst, recv_slot, device, of=None):
+    def send(src, dst, recv_slot, device, of=None, when=None):
         if not free:
             settle(len(pending) - 1)
         copy = pltpu.make_async_remote_copy(
@@ -183,8 +188,11 @@
             device_id=device,
             device_id_type=MESH,
         )
-        copy.start()
-        pending.append((copy, free.pop(0), of))
+        if when is None:
+            copy.start()
+        else:
+            pl.when(when)(copy.start)
+        pending.append((copy, free.pop(0), of, when))
 
     def arrived(dst, recv_slot):
         pltpu.make_async_remote_copy(
@@ -199,7 +207,10 @@
     def settle(keep=0, of=None):
         done = [p for p in pending if p[2] == of] if of else pending[: len(pending) - keep]
         for item in done:
-            item[0].wait_send()
+            if item[3] is None:
+                item[0].wait_send()
+            else:
+                pl.when(item[3])(item[0].wait_send)
             free.append(item[1])
         left = [p for p in pending if all(p is not q for q in done)]
         pending[:] = left
@@ -213,7 +224,7 @@
     def row_block(index):
         return pl.ds(pl.multiple_of(index * own, own), own)
 
-    nh = 2
+    nh = s.nh
     cut = own // nh
 
     def row_part(index, q):
@@ -227,6 +238,8 @@
     valid_row = (lax.broadcasted_iota(jnp.int32, (1, own), 1) < cnt_ref[0]).astype(FULL)
     counted = mask_ref[...].astype(FULL) * valid_row
 
+    prologue = jax.named_scope("prologue")
+    prologue.__enter__()
     pad = s.feat_up - up(s.feat, 16) + 16
     own_xt = xt_all.at[c]
     own_xt[s.feat_up - pad :, :] = jnp.zeros((pad, own), LOW)
@@ -240,6 +253,7 @@
 
     wide = [rslots(s.n_row * nh) for _ in range(2)]
     gbase = [rslots(s.n_col * nh) for _ in range(2)]
+    prologue.__exit__(None, None, None)
 
     def start_gather(hop, q, values):
         mine = v_all.at[hop, row_part(c, q)]
@@ -265,7 +279,8 @@
                         v_all.at[hop, row_part(source, q)], gbase[hop] + source * nh + q
                     )
 
-    pl.semaphore_wait(barrier, len(peers))
+    with jax.named_scope("barrier"):
+        pl.semaphore_wait(barrier, len(peers))
     for q in range(nh):
         start_gather(0, q, y1[q * cut : (q + 1) * cut])
 
@@ -297,17 +312,23 @@
                 "hop",
             )
 
+        sequence = []
+        for q in range(nh):
+            sequence += [(dz, q) for dz in order if dz]
+            if q:
+                sequence.append((0, q - 1))
+        sequence.append((0, nh - 1))
+        ready = set()
         with jax.named_scope("send_x"):
-            for dz in order:
+            for dz, q in sequence:
                 for dx in range(1, nx):
-                    place = (dx - 1) * nz + dz
-                    rt = zs(dz) * nx + xs(dx)
-                    xsend[place] = dot(tile[row_block(rt), :], v_all[hop]).astype(LOW)
-                    send_x(dz, dx, 0)
-            for q in range(1, nh):
-                for dz in order:
-                    for dx in range(1, nx):
-                        send_x(dz, dx, q)
+                    if (dz, dx) not in ready:
+                        ready.add((dz, dx))
+                        rt = zs(dz) * nx + xs(dx)
+                        xsend[(dx - 1) * nz + dz] = dot(
+                            tile[row_block(rt), :], v_all[hop]
+                        ).astype(LOW)
+                    send_x(dz, dx, q)
             for dz in order:
                 acc[:, dz * own : (dz + 1) * own] = dot(
                     tile[row_block(zs(dz) * nx + x), :], v_all[hop]
@@ -342,13 +363,13 @@
             finish(q, total)
 
         with jax.named_scope("send_z"):
-            for q in range(nh):
-                for i, dz in enumerate(order):
-                    totals[q] = send_z(dz, q)
-                    if q and i == nz // 2 - 1:
-                        with jax.named_scope("sum_z0"):
-                            sum_z(q - 1)
+            for dz, q in sequence[:-1]:
+                totals[q] = send_z(dz, q)
+                if not dz:
+                    with jax.named_scope("sum_z0"):
+                        sum_z(q)
         with jax.named_scope("sum_z1"):
+            totals[nh - 1] = send_z(0, nh - 1)
             sum_z(nh - 1)
 
     bias = [bias_ref[i * width : (i + 1) * width].reshape(1, width) for i in range(2)]
@@ -466,55 +487,83 @@
             else:
                 acc[:, j : j + step_cols] += here
 
+    def halves(lane, row):
+        return (
+            pl.ds(row * (width // 2), width // 2),
+            pl.ds(lane * (own // 2), own // 2),
+        )
+
+    quarters = [(lane, row) for lane in range(2) for row in range(2)]
+    relayed = nz == 4
+    inner = lax.rem((z + 1) // 2, 2) == 1
+
     def receive(hop, values, meanwhile=None):
         base = wide[hop]
         first = hop * s.n_row
-        pool[first] = values
-        for q in range(nh):
-            mine = pool.at[first, part(q)]
-            for dz in range(nz - 1, 0, -1):
-                send(
-                    mine,
-                    pool.at[first + dz, part(q)],
-                    base + dz * nh + q,
-                    at(zs(dz), x, y, k),
-                )
+
+        def piece(dz, dx, q):
+            return pool.at[(first + dx * nz + dz, *halves(*quarters[q]))]
+
+        def to_z(dz, q, when=None):
+            send(
+                piece(0, 0, q), piece(dz, 0, q), base + dz * nh + q, at(zs(dz), x, y, k), when=when
+            )
+
+        def to_x(dz, q):
             for dx in range(1, nx):
-                place = dx * nz
-                send(
-                    mine,
-                    pool.at[first + place, part(q)],
-                    base + place * nh + q,
-                    at(z, xs(dx), y, k),
-                )
+                place = dx * nz + dz
+                send(piece(dz, 0, q), piece(dz, dx, q), base + place * nh + q, at(z, xs(dx), y, k))
+
+        own_parts = []
+        for lane in range(2):
+            mine = values(lane)
+            own_parts.append(mine)
+            pool[first, :, lane * (own // 2) : (lane + 1) * (own // 2)] = mine
+            for q in (2 * lane, 2 * lane + 1):
+                if relayed:
+                    to_z(2, q, jnp.logical_not(inner))
+                    to_z(3, q, inner)
+                    to_z(1, q)
+                else:
+                    for dz in range(nz - 1, 0, -1):
+                        to_z(dz, q)
+                to_x(0, q)
 
         def source(dz, dx):
             return row_block(zback(dz) * nx + xs(nx - dx))
 
-        gained(values, row_block(r), fresh=True)
+        gained(jnp.concatenate(own_parts, axis=1), row_block(r), fresh=True)
         if meanwhile is not None:
             meanwhile()
-        for q in range(nh):
-            for dz in range(1, nz):
-                arrived(pool.at[first + dz, part(q)], base + dz * nh + q)
-                for dx in range(1, nx):
-                    place = dx * nz + dz
-                    send(
-                        pool.at[first + dz, part(q)],
-                        pool.at[first + place, part(q)],
-                        base + place * nh + q,
-                        at(z, xs(dx), y, k),
-                    )
-                if q == nh - 1:
-                    gained(pool[first + dz], source(dz, 0))
+
+        def step(dz, q):
+            arrived(piece(dz, 0, q), base + dz * nh + q)
+            if relayed and dz == 2:
+                send(piece(2, 0, q), piece(3, 0, q), base + 3 * nh + q, at(zs(1), x, y, k), when=inner)
+                to_z(2, q, inner)
+            to_x(dz, q)
+            if q == nh - 1:
+                gained(pool[first + dz], source(dz, 0))
+
+        if relayed:
+            for q in range(nh):
+                step(1, q)
+                step(2, q)
+                if q:
+                    step(3, q - 1)
+            step(3, nh - 1)
+        else:
+            for q in range(nh):
+                for dz in range(1, nz):
+                    step(dz, q)
         for dz in range(nz):
             for dx in range(1, nx):
-                place = dx * nz + dz
                 for q in range(nh):
-                    arrived(pool.at[first + place, part(q)], base + place * nh + q)
-                gained(pool[first + place], source(dz, dx))
+                    arrived(piece(dz, dx, q), base + (dx * nz + dz) * nh + q)
+                gained(pool[first + dx * nz + dz], source(dz, dx))
 
     dz2t = (dh2t * slope2t).astype(LOW)
+    half_own = own // 2
 
     def features_out():
         for d in range(1, ny):
@@ -524,42 +573,62 @@
 
     with jax.named_scope("back2_rows"):
         settle()
-        receive(0, dz2t, features_out)
+        receive(0, lambda lane: dz2t[:, lane * half_own : (lane + 1) * half_own], features_out)
+    cbase = rslots(2 * ny)
+    ybase = rslots(2 * ny)
+
+    def lane_part(index, lane):
+        return pl.ds(pl.multiple_of(index * own + lane * half_own, half_own), half_own)
+
+    def held(place, lane):
+        return xsend.at[place, :, pl.ds(lane * half_own, half_own)]
+
+    def crecv(dy, lane):
+        return v_all.at[0, dy * own : (dy + 1) * own, pl.ds(lane * half_own, half_own)]
+
+    def yrecv(dy, lane):
+        return crecv(dy + (ny if nk > 1 else 0), lane)
+
+    column_totals = [None, None]
     with jax.named_scope("back2_cols"):
-        cbase = rslots(ny)
-        ybase = rslots(ny)
-
-        def crecv(dy):
-            return v_all.at[0, dy * own : (dy + 1) * own]
-
-        def yrecv(dy):
-            return crecv(dy + (ny if nk > 1 else 0))
-
-        for dy in range(ny - 1, -1, -1):
-            if nk > 1:
-                xsend[dy] = acc[:, row_block(ys(dy) * nk + 1 - k)].astype(LOW)
-                send(xsend.at[dy], crecv(dy), cbase + dy, sibling)
-        total = dz2t.astype(FULL)
-        for dy in range(ny - 1, -1, -1):
-            here = acc[:, row_block(ys(dy) * nk + k)]
-            if nk > 1:
-                arrived(crecv(dy), cbase + dy)
-                here = here + crecv(dy)[...].astype(FULL)
-            if dy:
-                xsend[ny + dy] = here.astype(LOW)
-                send(xsend.at[ny + dy], yrecv(dy), ybase + dy, at(z, x, ys(dy), k))
-            else:
-                total = total + here
+        for lane in range(2):
+            for dy in range(ny - 1, -1, -1):
+                if nk > 1:
+                    there = held(dy, lane)
+                    there[...] = acc[:, lane_part(ys(dy) * nk + 1 - k, lane)].astype(LOW)
+                    send(there, crecv(dy, lane), cbase + 2 * dy + lane, sibling)
+        for lane in range(2):
+            for dy in range(ny - 1, -1, -1):
+                here = acc[:, lane_part(ys(dy) * nk + k, lane)]
+                if nk > 1:
+                    arrived(crecv(dy, lane), cbase + 2 * dy + lane)
+                    here = here + crecv(dy, lane)[...].astype(FULL)
+                if dy:
+                    there = held(ny + dy, lane)
+                    there[...] = here.astype(LOW)
+                    send(
+                        there, yrecv(dy, lane), ybase + 2 * dy + lane, at(z, x, ys(dy), k)
+                    )
+                else:
+                    column_totals[lane] = here
         for d in range(1, ny):
             source = ys(ny - d) * nk + k
             arrived(xt_all.at[source], xt_base + source)
             if nk > 1:
                 send(xt_all.at[source], xt_all.at[source], xt_base + source, sibling)
-        for dy in range(1, ny):
-            arrived(yrecv(dy), ybase + dy)
-            total = total + yrecv(dy)[...].astype(FULL)
-    dy2t = total.astype(LOW)
-    dz1t = (dot(w2, dy2t) * slope1t).astype(LOW)
+
+    dy2_parts, dz1_parts = [], []
+
+    def first_slopes(lane):
+        lanes_q = slice(lane * half_own, (lane + 1) * half_own)
+        total = column_totals[lane] + dz2t[:, lanes_q].astype(FULL)
+        with jax.named_scope("y_wait"):
+            for dy in range(1, ny):
+                arrived(yrecv(dy, lane), ybase + 2 * dy + lane)
+                total = total + yrecv(dy, lane)[...].astype(FULL)
+        dy2_parts.append(total.astype(LOW))
+        dz1_parts.append((dot(w2, dy2_parts[lane]) * slope1t[:, lanes_q]).astype(LOW))
+        return dz1_parts[lane]
 
     lanes, plane = s.lanes, s.plane
     me = y * nx + x
@@ -644,12 +713,14 @@
                 for i in range(plane):
                     arrived(fin.at[1 - k, self.piece(i)], base + plane + i)
 
-    one = Total(0, s.one_rows)
+    one_a = Total(0, s.cut_rows)
+    one_b = Total(s.cut_rows, s.one_rows - s.cut_rows)
     two = Total(s.one_rows, s.two_rows)
     tail = s.two_rows - width - s.cls
 
     def early():
         grad3t = dot(qt, h2)
+        dy2t = jnp.concatenate(dy2_parts, axis=1)
         grad2 = dot_nt(h1t, dy2t)
         acc_two = jnp.concatenate(
             [grad2, grad3t] + ([jnp.zeros((tail, width), FULL)] if tail else []), axis=0
@@ -663,30 +734,34 @@
             two.plane_send(acc_two)
 
     with jax.named_scope("back1_rows"):
-        receive(1, dz1t, early)
+        receive(1, first_slopes, early)
     with jax.named_scope("grad1"):
         two.line_send()
+        dz1t = jnp.concatenate(dz1_parts, axis=1)
         acc[:, row_block(c)] += dz1t.astype(FULL)
         if nk > 1:
             for d in range(ny):
                 source = ys(d) * nk + 1 - k
                 arrived(xt_all.at[source], xt_base + source)
 
-        def grad_one(index):
+        def grad_one(index, start, stop):
             total = None
+            end = min(stop, s.feat_up)
             for i in range(s.n_col):
                 here = acc[pl.ds(pl.multiple_of(index * lanes, lanes), lanes), :]
-                here = dot_nt(xt_all[i], here[:, i * own : (i + 1) * own].astype(LOW))
+                here = dot_nt(
+                    xt_all[i, start:end, :], here[:, i * own : (i + 1) * own].astype(LOW)
+                )
                 total = here if total is None else total + here
-            if s.one_rows <= s.feat_up:
-                return total[: s.one_rows]
-            return jnp.concatenate(
-                [total, jnp.zeros((s.one_rows - s.feat_up, lanes), FULL)], axis=0
-            )
+            if end < stop:
+                total = jnp.concatenate([total, jnp.zeros((stop - end, lanes), FULL)], axis=0)
+            return total
 
         if nk > 1:
-            one.core_send(grad_one(1 - k))
-        mine_one = grad_one(k)
+            one_a.core_send(grad_one(1 - k, 0, s.cut_rows))
+            one_b.core_send(grad_one(1 - k, s.cut_rows, s.one_rows))
+        one_a.plane_send(grad_one(k, 0, s.cut_rows))
+        one_b.plane_send(grad_one(k, s.cut_rows, s.one_rows))
         ones = jnp.ones((8, own), LOW)
         line = lax.broadcasted_iota(jnp.int32, (8, width), 0)
         lane = lax.broadcasted_iota(jnp.int32, (8, width), 1)
@@ -702,7 +777,6 @@
             send(misc_k.at[0], misc_k.at[1], mbase, sibling)
 
     with jax.named_scope("sum_plane"):
-        one.plane_send(mine_one)
         if nk > 1:
             arrived(misc_k.at[1], mbase)
             misc = misc_k[0] + misc_k[1]
@@ -713,7 +787,8 @@
         left = len(pending)
         two.back_send()
     with jax.named_scope("sum_line"):
-        one.line_send()
+        one_a.line_send()
+        one_b.line_send()
         for dx, dy in others:
             there = ys(dy) * nx + xs(dx)
             arrived(misc_p.at[there], mbase + there)
@@ -728,7 +803,8 @@
         two.end()
         settle(len(pending) - left)
     with jax.named_scope("back_line"):
-        one.back_send()
+        one_a.back_send()
+        one_b.back_send()
         for dz in range(1, nz):
             arrived(misc_z.at[zback(dz)], mbase + zback(dz))
         misc = misc_z[0]
@@ -737,47 +813,103 @@
         misc_ref[...] = jnp.where(line == 4, 1.0 / misc[3:4, 1:2], misc)
         grad_ref[:, s.one_rows :, :] = fin[:, s.one_rows :, :]
     with jax.named_scope("back_plane"):
-        one.back_forward()
-        one.end()
+        one_a.back_forward()
+        one_b.back_forward()
+        one_a.end()
+        one_b.end()
         grad_ref[:, : s.one_rows, :] = fin[:, : s.one_rows, :]
     with jax.named_scope("settle"):
         settle()
     assert rcount[0] <= s.arrivals
 
 
-def adam_kernel(
-    s, grad_ref, misc_ref, *refs
-):
-    ins, outs = refs[:12], refs[12:]
-    width, classes, f = s.width, s.classes, s.one_rows
+def update_pieces(s):
+    middle = up(s.feat // 2, 8)
+    return (
+        (0, 0, middle),
+        (0, middle, s.feat - middle),
+        (1, 0, s.width),
+        (2, 0, s.classes),
+    )
+
+
+def adam_kernel(s, grad_hbm, misc_hbm, *refs):
+    ins, outs, scratch = refs[:12], refs[12:26], refs[26:]
+    grad_ref, misc_ref, bias_in, bias_out, ends, *held = scratch[:-2]
+    sem_in, sem_out = scratch[-2:]
+    pieces = update_pieces(s)
+    width, classes, lanes = s.width, s.classes, s.lanes
+    grad_at = (0, s.one_rows, s.one_rows + width)
+
+    misc_load = pltpu.make_async_copy(misc_hbm, misc_ref, sem_in.at[0])
+    grad_load = pltpu.make_async_copy(grad_hbm, grad_ref, sem_in.at[1])
+    misc_load.start()
+    grad_load.start()
+    loads, count = [], 2
+    for n, (which, start, rows) in enumerate(pieces):
+        mine = []
+        for i in range(3):
+            mine.append(
+                pltpu.make_async_copy(
+                    ins[3 * which + i].at[pl.ds(start, rows)], held[2 * n].at[i], sem_in.at[count]
+                )
+            )
+            count += 1
+            mine[-1].start()
+        loads.append(mine)
+    bias_loads = []
+    for i in range(3):
+        bias_loads.append(
+            pltpu.make_async_copy(ins[9 + i], bias_in[i], sem_in.at[count])
+        )
+        count += 1
+        bias_loads[-1].start()
+
+    misc_load.wait()
+    grad_load.wait()
     total = misc_ref[3:4, 1:2]
     scale = misc_ref[4:5, 0:1]
-    lanes = s.lanes
-
-    def update(place, rows, lane, grad):
-        weight, first, second = (ins[3 * place + i][rows, lane] for i in range(3))
-        new = adam_update(weight, first, second, grad * scale)
-        for i in range(3):
-            outs[3 * place + i][rows, lane] = new[i]
-
-    for i in range(s.nk):
-        lane = slice(i * lanes, (i + 1) * lanes)
-        update(0, slice(0, s.feat), lane, grad_ref[i, : s.feat, :].astype(FULL))
-        update(1, slice(0, width), lane, grad_ref[i, f : f + width, :].astype(FULL))
-        update(
-            2,
-            slice(0, classes),
-            lane,
-            grad_ref[i, f + width : f + width + s.cls, :].astype(FULL)[:classes],
-        )
+    stores, count = [], 2
+    ends[0] = misc_ref[3:4, 0:1]
+    ends[1] = total
+    for i in range(2):
+        stores.append(pltpu.make_async_copy(ends.at[i], outs[12 + i], sem_out.at[i]))
+        stores[-1].start()
+    for n, (which, start, rows) in enumerate(pieces):
+        for load in loads[n]:
+            load.wait()
+        source, target = held[2 * n], held[2 * n + 1]
+        for i in range(s.nk):
+            lane = slice(i * lanes, (i + 1) * lanes)
+            first = grad_at[which] + start
+            grad = grad_ref[i, first : first + up(rows, 16), :].astype(FULL)[:rows]
+            weight, one, two = (source[j, :, lane] for j in range(3))
+            for j, new in enumerate(adam_update(weight, one, two, grad * scale)):
+                target[j, :, lane] = new
+        for j in range(3):
+            stores.append(
+                pltpu.make_async_copy(
+                    target.at[j], outs[3 * which + j].at[pl.ds(start, rows)], sem_out.at[count]
+                )
+            )
+            count += 1
+            stores[-1].start()
+    for load in bias_loads:
+        load.wait()
     for i, size in enumerate((width, width, classes)):
         span = slice(i * width, i * width + size)
-        weight, first, second = (ins[9 + j][span] for j in range(3))
+        weight, first, second = (bias_in[j][span] for j in range(3))
         new = adam_update(weight, first, second, misc_ref[i, :size] * misc_ref[4, :size])
         for j in range(3):
-            outs[9 + j][span] = new[j]
-    outs[12][...] = misc_ref[3:4, 0:1]
-    outs[13][...] = total
+            bias_out[j][span] = new[j]
+    for j in range(3):
+        stores.append(
+            pltpu.make_async_copy(bias_out[j], outs[9 + j], sem_out.at[count])
+        )
+        count += 1
+        stores[-1].start()
+    for store in stores:
+        store.wait()
 
 
 def shards(
@@ -809,6 +941,7 @@
     lanes = s.lanes
     vmem = pl.BlockSpec(memory_space=pltpu.VMEM)
     smem = pl.BlockSpec(memory_space=pltpu.SMEM)
+    anywhere = pl.BlockSpec(memory_space=pl.ANY)
     block = (own, width)
     small = (s.cls, own)
     shapes = [
@@ -848,7 +981,7 @@
         ),
         in_specs=[
             vmem,
-            pl.BlockSpec(memory_space=pl.ANY),
+            anywhere,
             smem,
             vmem,
             vmem,
@@ -905,8 +1038,22 @@
             jax.ShapeDtypeStruct((1, 1), FULL),
             jax.ShapeDtypeStruct((1, 1), FULL),
         ),
-        in_specs=[vmem] * 14,
-        out_specs=(vmem,) * 14,
+        in_specs=[anywhere] * 14,
+        out_specs=(anywhere,) * 14,
+        scratch_shapes=[
+            pltpu.VMEM(grads.shape, LOW),
+            pltpu.VMEM(misc.shape, FULL),
+            [pltpu.VMEM(biases.shape, FULL)] * 3,
+            [pltpu.VMEM(biases.shape, FULL)] * 3,
+            pltpu.VMEM((2, 1, 1), FULL),
+            *[
+                pltpu.VMEM((3, rows, width), FULL)
+                for _, _, rows in update_pieces(s)
+                for _ in range(2)
+            ],
+            pltpu.SemaphoreType.DMA((17,)),
+            pltpu.SemaphoreType.DMA((17,)),
+        ],
         compiler_params=pltpu.CompilerParams(vmem_limit_bytes=62 * 2**20),
         name="update",
     )(grads, misc, *state)

time: 137 us -> 130 us (0.949)
  Pallas kernels: 136 us -> 128 us
    pallas_call x1, Pallas kernels: 132 us -> 125 us  [shards(): pl.pallas_call(functools.partial(kernel, s), out_shape=(jax.ShapeDtypeStr...]
where the time goes in v2:
time: 130 us
  Pallas kernels  128 us (98%)
  between operations  1.3 us (1%)
    pallas_call x1, Pallas kernels, shards(): pl.pallas_call(functools.partial(kernel, s), out_shape=(jax.ShapeDtypeStr...  125 us
    pallas_call x1, Pallas kernels, shards(): pl.pallas_call(functools.partial(adam_kernel, s), out_shape=(*[jax.ShapeD...  3.63 us

profile of v2, /device:TPU:0, one launch (start us, length us, event | category | flops | bytes accessed | tf_op | source)
XLA Modules:
  0.0 129.5 jit_solution(4373930634069266420)
XLA Ops:
  1.3 124.6 %step.1 = (bf16[2,960,128]{2,1,0:T(8,128)(2,1)}, f32[8,256]{1,0:T(8,128)}) custom-call(bf16[602,256]{1,0:T(8,128)(2,1)} %bitcast.15, bf16[2048,1024]{1,0:T(8,128)(2,1)} %adj_ref.1, s32[4,4]{1,0:T(4,128)} %occ_ref.1, s32[1,256]{1,0:T(1,128)} %bitcast.19, s32[1,256]{1,0:T(1,128)} %bitcast.20, s32[1]{0:T(128)S(6)} %copy.32.cnt_ref, f32[602,256]{1,0:T(8,128)} %refs_0_.1, ...), custom_call_target="tpu_custom_call" | custom-call | flops 6442450944 | bytes 4194304 | tf_op jit(solution)/shard_map/step/pallas_call | solution.py:976
  125.9 3.6 %update.1 = (f32[602,256]{1,0:T(8,128)}, f32[602,256]{1,0:T(8,128)}, f32[602,256]{1,0:T(8,128)}, f32[256,256]{1,0:T(8,128)}, f32[256,256]{1,0:T(8,128)}, /*index...) custom-call(bf16[2,960,128]{2,1,0:T(8,128)(2,1)} %get-tuple-element., ...), custom_call_target="tpu_custom_call" | custom-call | tf_op jit(solution)/shard_map/update/pallas_call | solution.py:1034

commit v3 on v2

--- a/solution.py
+++ b/solution.py
@@ -72,10 +72,10 @@
         units = self.one_rows // (16 * self.plane)
         self.cut_rows = (units + 1) // 2 * 16 * self.plane
         self.nh = 4
+        self.relayed = self.nz == 4
         self.sends = 3 * (n_row + n_col) + 3 * self.plane
         wide = 2 * self.nh * (n_row + n_col)
-        self.arrivals = wide + 2 * (n_row + n_col) + n_col + 4 * self.ny
-        self.arrivals += 3 * (1 + 3 * self.plane + self.nz) + 1 + self.plane + self.nz
+        self.arrivals = wide + 3 * (1 + 3 * self.plane + self.nz) + 1 + self.plane + self.nz
 
 
 def kernel(
@@ -150,6 +150,17 @@
         return zs(d) if not nz & (nz - 1) else lax.rem(z + nz - d, nz)
 
     sibling = at(z, x, y, 1 - k)
+    relayed = s.relayed
+    is_inner = lax.rem((z + 1) // 2, 2)
+    inner = is_inner == 1
+    outer = is_inner == 0
+    line = [dz for dz in range(nz - 1, -1, -1)]
+    row_far = [(dz, dx) for dz in line for dx in range(nx - 1, -1, -1) if dz or dx]
+    col_far = [(dy, dk) for dy in range(ny - 1, -1, -1) for dk in range(nk - 1, -1, -1) if dy or dk]
+
+    def ks(d):
+        return lax.rem(k + d, nk)
+
 
     rows, cols = tile.shape
     n_sub = rows // SUB
@@ -177,7 +188,7 @@
     free = list(range(s.sends))
     pending = []
 
-    def send(src, dst, recv_slot, device, of=None, when=None):
+    def send(src, dst, recv_slot, device, of=None, when=None, start=True):
         if not free:
             settle(len(pending) - 1)
         copy = pltpu.make_async_remote_copy(
@@ -188,11 +199,13 @@
             device_id=device,
             device_id_type=MESH,
         )
-        if when is None:
-            copy.start()
-        else:
-            pl.when(when)(copy.start)
+        if start:
+            if when is None:
+                copy.start()
+            else:
+                pl.when(when)(copy.start)
         pending.append((copy, free.pop(0), of, when))
+        return copy
 
     def arrived(dst, recv_slot):
         pltpu.make_async_remote_copy(
@@ -284,6 +297,12 @@
     for q in range(nh):
         start_gather(0, q, y1[q * cut : (q + 1) * cut])
 
+    if relayed:
+
+        @pl.when(outer)
+        def _():
+            zrecv[:, 2] = jnp.zeros((2, own, width), LOW)
+
     w3t[...] = jnp.zeros_like(w3t)
     w3t[: s.classes, :] = w3t_ref[...].astype(LOW)
     w2 = w2_ref[...].astype(LOW)
@@ -313,11 +332,19 @@
             )
 
         sequence = []
-        for q in range(nh):
-            sequence += [(dz, q) for dz in order if dz]
-            if q:
-                sequence.append((0, q - 1))
-        sequence.append((0, nh - 1))
+        if relayed:
+            for q in range(nh):
+                sequence.append((3, q))
+                if q:
+                    sequence.append((2, q - 1))
+            sequence += [(dz, q) for dz, q in ((2, nh - 1),)]
+            sequence += [(dz, q) for dz in (1, 0) for q in range(nh)]
+        else:
+            for q in range(nh):
+                sequence += [(dz, q) for dz in order if dz]
+                if q:
+                    sequence.append((0, q - 1))
+            sequence.append((0, nh - 1))
         ready = set()
         with jax.named_scope("send_x"):
             for dz, q in sequence:
@@ -341,15 +368,33 @@
                 place = (dx - 1) * nz + dz
                 arrived(pool.at[hop * s.n_row + place, part(q)], xbase + place * nh + q)
                 total = total + pool[hop * s.n_row + place, rows_q, :].astype(FULL)
-            if dz:
+            if not dz:
+                return total
+            there, slot, mark = zs(dz), dz - 1, zbase + dz * nh + q
+            if relayed and dz == 3:
+                there = is_inner * zs(3) + (1 - is_inner) * zs(1)
+                slot, mark = 3 - is_inner, zbase + 3 * nh * is_inner + q
+            if relayed and dz == 2:
+
+                @pl.when(inner)
+                def _():
+                    arrived(zrecv.at[hop, 3, part(q)], zbase + q)
+                    handed = zrecv[hop, 3, rows_q, :].astype(FULL)
+                    zsend[dz - 1, rows_q, :] = (total + handed).astype(LOW)
+
+                @pl.when(outer)
+                def _():
+                    zsend[dz - 1, rows_q, :] = total.astype(LOW)
+
+            else:
                 zsend[dz - 1, rows_q, :] = total.astype(LOW)
-                send(
-                    zsend.at[dz - 1, part(q)],
-                    zrecv.at[hop, dz - 1, part(q)],
-                    zbase + dz * nh + q,
-                    at(zs(dz), x, y, k),
-                    "hop",
-                )
+            send(
+                zsend.at[dz - 1, part(q)],
+                zrecv.at[hop, slot, part(q)],
+                mark,
+                at(there, x, y, k),
+                "hop",
+            )
             return total
 
         totals = [None] * nh
@@ -358,7 +403,11 @@
             total = totals[q]
             rows_q = slice(q * cut, (q + 1) * cut)
             for dz in range(1, nz):
-                arrived(zrecv.at[hop, dz - 1, part(q)], zbase + dz * nh + q)
+                there, mark = zrecv.at[hop, dz - 1, part(q)], zbase + dz * nh + q
+                if relayed and dz == 3:
+                    pl.when(inner)(functools.partial(arrived, there, mark))
+                else:
+                    arrived(there, mark)
                 total = total + zrecv[hop, dz - 1, rows_q, :].astype(FULL)
             finish(q, total)
 
@@ -387,7 +436,7 @@
     h1t = jnp.concatenate(acts, axis=0).astype(FULL).T.astype(LOW)
     slope1t = jnp.concatenate(slopes, axis=0).T
 
-    xt_base = rslots(s.n_col)
+    xt_base = gbase[1] + s.n_col
 
     def second_done(q, total):
         rows_q = slice(q * cut, (q + 1) * cut)
@@ -401,30 +450,29 @@
     y3t = dot_nt(w3t[...], h2).astype(LOW)
 
     with jax.named_scope("hop3_gather"):
-        base = rslots(s.n_col)
+        base = gbase[0]
         mine = v3_all.at[c]
         mine[...] = y3t
-        for d in range(1, s.n_col):
-            send(mine, mine, base + c, (r, lax.rem(c + d, s.n_col)))
+        for dy, dk in col_far:
+            send(mine, mine, base + c, (r, ys(dy) * nk + ks(dk)))
         slope2t = jnp.concatenate(slopes, axis=0).T
         settle(s.n_col - 1)
-        for d in range(1, s.n_col):
-            source = lax.rem(c + d, s.n_col)
+        for dy, dk in reversed(col_far):
+            source = ys(ny - dy) * nk + ks(nk - dk)
             arrived(v3_all.at[source], base + source)
     with jax.named_scope("hop3_sum"):
-        pbase = rslots(s.n_row)
+        pbase = wide[0]
         v3 = jnp.concatenate([v3_all[i] for i in range(s.n_col)], axis=1)
-        for d in range(s.n_row - 1, -1, -1):
-            rt = lax.rem(r + d, s.n_row)
-            here = dot_nt(v3, tile[row_block(rt), :])
-            if d:
-                p3send[d - 1] = here.astype(LOW)
-                send(p3send.at[d - 1], p3recv.at[d - 1], pbase + d, (rt, c))
-            else:
-                total = here
-        for d in range(1, s.n_row):
-            arrived(p3recv.at[d - 1], pbase + d)
-            total = total + p3recv[d - 1].astype(FULL)
+        for dz, dx in row_far:
+            place = dz * nx + dx
+            rt = zs(dz) * nx + xs(dx)
+            p3send[place] = dot_nt(v3, tile[row_block(rt), :]).astype(LOW)
+            send(p3send.at[place], p3recv.at[place], pbase + place, (rt, c))
+        total = dot_nt(v3, tile[row_block(r), :])
+        for dz, dx in reversed(row_far):
+            place = dz * nx + dx
+            arrived(p3recv.at[place], pbase + place)
+            total = total + p3recv[place].astype(FULL)
     total = total + y3t.astype(FULL)
 
     place = lax.broadcasted_iota(jnp.int32, (s.cls, own), 0)
@@ -448,31 +496,29 @@
     dlt = ((weight / norm - target) * counted).astype(LOW)
 
     with jax.named_scope("back3_gather"):
-        base = rslots(s.n_row)
+        base = wide[1]
         mine = dl_all.at[r]
         mine[...] = dlt
-        for d in range(s.n_row - 1, 0, -1):
-            send(mine, mine, base + r, (lax.rem(r + d, s.n_row), c))
+        for dz, dx in row_far:
+            send(mine, mine, base + r, (zs(dz) * nx + xs(dx), c))
         here = dot(dlt, tile[row_block(r), :])
-        for d in range(1, s.n_row):
-            source = lax.rem(r + d, s.n_row)
+        for dz, dx in reversed(row_far):
+            source = zback(dz) * nx + xs(nx - dx)
             arrived(dl_all.at[source], base + source)
             here = here + dot(dl_all[source], tile[row_block(source), :])
         acc[: s.cls, :cols] = here
     with jax.named_scope("back3_sum"):
-        qbase = rslots(s.n_col)
-        total = dlt.astype(FULL)
-        for d in range(s.n_col - 1, -1, -1):
-            ct = lax.rem(c + d, s.n_col)
-            here = acc[: s.cls, row_block(ct)]
-            if d:
-                q3send[d - 1] = here.astype(LOW)
-                send(q3send.at[d - 1], q3recv.at[d - 1], qbase + d, (r, ct))
-            else:
-                total = total + here
-        for d in range(1, s.n_col):
-            arrived(q3recv.at[d - 1], qbase + d)
-            total = total + q3recv[d - 1].astype(FULL)
+        qbase = gbase[1]
+        for dy, dk in col_far:
+            place = dy * nk + dk
+            ct = ys(dy) * nk + ks(dk)
+            q3send[place] = acc[: s.cls, row_block(ct)].astype(LOW)
+            send(q3send.at[place], q3recv.at[place], qbase + place, (r, ct))
+        total = dlt.astype(FULL) + acc[: s.cls, row_block(c)]
+        for dy, dk in reversed(col_far):
+            place = dy * nk + dk
+            arrived(q3recv.at[place], qbase + place)
+            total = total + q3recv[place].astype(FULL)
     qt = total.astype(LOW)
     dh2t = lax.dot_general(
         w3t[...], qt, (((0,), (0,)), ((), ())), preferred_element_type=FULL
@@ -494,25 +540,34 @@
         )
 
     quarters = [(lane, row) for lane in range(2) for row in range(2)]
-    relayed = nz == 4
-    inner = lax.rem((z + 1) // 2, 2) == 1
-
-    def receive(hop, values, meanwhile=None):
+    def receive(hop, values, meanwhile=None, late=None):
         base = wide[hop]
         first = hop * s.n_row
 
         def piece(dz, dx, q):
             return pool.at[(first + dx * nz + dz, *halves(*quarters[q]))]
 
-        def to_z(dz, q, when=None):
-            send(
-                piece(0, 0, q), piece(dz, 0, q), base + dz * nh + q, at(zs(dz), x, y, k), when=when
+        def to_z(dz, q, when=None, start=True):
+            return send(
+                piece(0, 0, q),
+                piece(dz, 0, q),
+                base + dz * nh + q,
+                at(zs(dz), x, y, k),
+                when=when,
+                start=start,
             )
 
-        def to_x(dz, q):
-            for dx in range(1, nx):
-                place = dx * nz + dz
-                send(piece(dz, 0, q), piece(dz, dx, q), base + place * nh + q, at(z, xs(dx), y, k))
+        def to_x(dz, q, start=True):
+            return [
+                send(
+                    piece(dz, 0, q),
+                    piece(dz, dx, q),
+                    base + (dx * nz + dz) * nh + q,
+                    at(z, xs(dx), y, k),
+                    start=start,
+                )
+                for dx in range(1, nx)
+            ]
 
         own_parts = []
         for lane in range(2):
@@ -521,8 +576,7 @@
             pool[first, :, lane * (own // 2) : (lane + 1) * (own // 2)] = mine
             for q in (2 * lane, 2 * lane + 1):
                 if relayed:
-                    to_z(2, q, jnp.logical_not(inner))
-                    to_z(3, q, inner)
+                    to_z(2, q)
                     to_z(1, q)
                 else:
                     for dz in range(nz - 1, 0, -1):
@@ -536,26 +590,62 @@
         if meanwhile is not None:
             meanwhile()
 
+        passing = {
+            (dz, q): to_x(dz, q, start=False) for q in range(nh) for dz in range(1, nz)
+        }
+
         def step(dz, q):
             arrived(piece(dz, 0, q), base + dz * nh + q)
-            if relayed and dz == 2:
-                send(piece(2, 0, q), piece(3, 0, q), base + 3 * nh + q, at(zs(1), x, y, k), when=inner)
-                to_z(2, q, inner)
-            to_x(dz, q)
-            if q == nh - 1:
-                gained(pool[first + dz], source(dz, 0))
+            for copy in passing[dz, q]:
+                copy.start()
 
         if relayed:
-            for q in range(nh):
-                step(1, q)
-                step(2, q)
-                if q:
-                    step(3, q - 1)
-            step(3, nh - 1)
+            relays = [
+                send(
+                    piece(2, 0, q),
+                    piece(3, 0, q),
+                    base + 3 * nh + q,
+                    at(zs(1), x, y, k),
+                    when=inner,
+                    start=False,
+                )
+                for q in range(nh)
+            ]
+            paced = [to_z(3, q, inner, start=False) for q in range(nh)]
+
+            @pl.when(inner)
+            def _():
+                for q in range(nh):
+                    arrived(piece(2, 0, q), base + 2 * nh + q)
+                    relays[q].start()
+                    paced[q].start()
+                    for copy in passing[2, q]:
+                        copy.start()
+                    step(1, q)
+                    if q > 1:
+                        step(3, q - 2)
+                for q in range(nh - 2, nh):
+                    step(3, q)
+
+            @pl.when(outer)
+            def _():
+                for q in range(nh + 2):
+                    if q < nh:
+                        step(1, q)
+                    if 0 < q <= nh:
+                        step(2, q - 1)
+                    if q > 2:
+                        step(3, q - 3)
+                for q in range(nh - 1, nh):
+                    step(3, q)
         else:
             for q in range(nh):
                 for dz in range(1, nz):
                     step(dz, q)
+        for dz in range(1, nz):
+            gained(pool[first + dz], source(dz, 0))
+        if late is not None:
+            late()
         for dz in range(nz):
             for dx in range(1, nx):
                 for q in range(nh):
@@ -574,8 +664,8 @@
     with jax.named_scope("back2_rows"):
         settle()
         receive(0, lambda lane: dz2t[:, lane * half_own : (lane + 1) * half_own], features_out)
-    cbase = rslots(2 * ny)
-    ybase = rslots(2 * ny)
+    cbase = gbase[0] + s.n_col
+    ybase = gbase[1] + 2 * s.n_col
 
     def lane_part(index, lane):
         return pl.ds(pl.multiple_of(index * own + lane * half_own, half_own), half_own)
@@ -713,6 +803,16 @@
                 for i in range(plane):
                     arrived(fin.at[1 - k, self.piece(i)], base + plane + i)
 
+    written = []
+
+    def write(start, count):
+        rows_w = pl.ds(start, count)
+        copy = pltpu.make_async_copy(
+            fin.at[:, rows_w], grad_ref.at[:, rows_w], lsem.at[n_sub + len(written)]
+        )
+        copy.start()
+        written.append(copy)
+
     one_a = Total(0, s.cut_rows)
     one_b = Total(s.cut_rows, s.one_rows - s.cut_rows)
     two = Total(s.one_rows, s.two_rows)
@@ -734,9 +834,8 @@
             two.plane_send(acc_two)
 
     with jax.named_scope("back1_rows"):
-        receive(1, first_slopes, early)
+        receive(1, first_slopes, early, two.line_send)
     with jax.named_scope("grad1"):
-        two.line_send()
         dz1t = jnp.concatenate(dz1_parts, axis=1)
         acc[:, row_block(c)] += dz1t.astype(FULL)
         if nk > 1:
@@ -763,14 +862,14 @@
         one_a.plane_send(grad_one(k, 0, s.cut_rows))
         one_b.plane_send(grad_one(k, s.cut_rows, s.one_rows))
         ones = jnp.ones((8, own), LOW)
-        line = lax.broadcasted_iota(jnp.int32, (8, width), 0)
+        row = lax.broadcasted_iota(jnp.int32, (8, width), 0)
         lane = lax.broadcasted_iota(jnp.int32, (8, width), 1)
         bias_three = jnp.concatenate([dlt, jnp.zeros((width - s.cls, own), LOW)], axis=0)
-        misc = jnp.where(line == 0, dot_nt(ones, dz1t), 0.0)
-        misc = jnp.where(line == 1, dot_nt(ones, dz2t), misc)
-        misc = jnp.where(line == 2, dot_nt(ones, bias_three), misc)
-        misc = jnp.where((line == 3) & (lane == 0), loss, misc)
-        misc = jnp.where((line == 3) & (lane == 1), number, misc)
+        misc = jnp.where(row == 0, dot_nt(ones, dz1t), 0.0)
+        misc = jnp.where(row == 1, dot_nt(ones, dz2t), misc)
+        misc = jnp.where(row == 2, dot_nt(ones, bias_three), misc)
+        misc = jnp.where((row == 3) & (lane == 0), loss, misc)
+        misc = jnp.where((row == 3) & (lane == 1), number, misc)
         mbase = rslots(1 + plane + nz)
         misc_k[0] = misc
         if nk > 1:
@@ -810,16 +909,23 @@
         misc = misc_z[0]
         for i in range(1, nz):
             misc = misc + misc_z[i]
-        misc_ref[...] = jnp.where(line == 4, 1.0 / misc[3:4, 1:2], misc)
-        grad_ref[:, s.one_rows :, :] = fin[:, s.one_rows :, :]
+        misc_k[0] = jnp.where(row == 4, 1.0 / misc[3:4, 1:2], misc)
+        written.append(
+            pltpu.make_async_copy(misc_k.at[0], misc_ref.at[pl.ds(0, 8)], lsem.at[n_sub])
+        )
+        written[0].start()
+        write(s.one_rows, s.two_rows)
     with jax.named_scope("back_plane"):
         one_a.back_forward()
         one_b.back_forward()
         one_a.end()
+        write(0, s.cut_rows)
         one_b.end()
-        grad_ref[:, : s.one_rows, :] = fin[:, : s.one_rows, :]
+        write(s.cut_rows, s.one_rows - s.cut_rows)
     with jax.named_scope("settle"):
         settle()
+        for copy in written:
+            copy.wait()
     assert rcount[0] <= s.arrivals
 
 
@@ -841,8 +947,10 @@
     width, classes, lanes = s.width, s.classes, s.lanes
     grad_at = (0, s.one_rows, s.one_rows + width)
 
-    misc_load = pltpu.make_async_copy(misc_hbm, misc_ref, sem_in.at[0])
-    grad_load = pltpu.make_async_copy(grad_hbm, grad_ref, sem_in.at[1])
+    misc_load = pltpu.make_async_copy(misc_hbm.at[pl.ds(0, 8)], misc_ref, sem_in.at[0])
+    grad_load = pltpu.make_async_copy(
+        grad_hbm.at[:, pl.ds(0, s.grad_rows)], grad_ref, sem_in.at[1]
+    )
     misc_load.start()
     grad_load.start()
     loads, count = [], 2
@@ -953,7 +1061,7 @@
         ((2 * s.n_row, *block), LOW),
         ((max(2 * s.ny, s.n_row - s.nz), *block), LOW),
         ((max(1, s.nz - 1), *block), LOW),
-        ((2, max(1, s.nz - 1), *block), LOW),
+        ((2, s.nz if s.relayed else max(1, s.nz - 1), *block), LOW),
         ((s.n_col, *small), LOW),
         ((s.n_row, *small), LOW),
         ((s.n_row, *small), LOW),
@@ -991,12 +1099,12 @@
             vmem,
             vmem,
         ],
-        out_specs=(vmem, vmem),
+        out_specs=(anywhere, anywhere),
         scratch_shapes=[
             *[pltpu.VMEM(shape, kind) for shape, kind in shapes],
             pltpu.SemaphoreType.DMA((s.sends,)),
             pltpu.SemaphoreType.DMA((s.arrivals,)),
-            pltpu.SemaphoreType.DMA((rows // SUB,)),
+            pltpu.SemaphoreType.DMA((rows // SUB + 4,)),
         ],
         compiler_params=pltpu.CompilerParams(
             collective_id=0, has_side_effects=True, vmem_limit_bytes=limit
@@ -1041,8 +1149,8 @@
         in_specs=[anywhere] * 14,
         out_specs=(anywhere,) * 14,
         scratch_shapes=[
-            pltpu.VMEM(grads.shape, LOW),
-            pltpu.VMEM(misc.shape, FULL),
+            pltpu.VMEM((s.nk, s.grad_rows, lanes), LOW),
+            pltpu.VMEM((8, width), FULL),
             [pltpu.VMEM(biases.shape, FULL)] * 3,
             [pltpu.VMEM(biases.shape, FULL)] * 3,
             pltpu.VMEM((2, 1, 1), FULL),

time: 130 us -> 123 us (0.946)
  Pallas kernels: 128 us -> 121 us
    pallas_call x1, Pallas kernels: 125 us -> 117 us  [shards(): pl.pallas_call(functools.partial(kernel, s), out_shape=(jax.ShapeDtypeStr...]
where the time goes in v3:
time: 123 us; the launch traced here: 122 us
  Pallas kernels  121 us (98%)
  between operations  1.46 us (1%)
    pallas_call x1, Pallas kernels, shards(): pl.pallas_call(functools.partial(kernel, s), out_shape=(jax.ShapeDtypeStr...  117 us
    pallas_call x1, Pallas kernels, shards(): pl.pallas_call(functools.partial(adam_kernel, s), out_shape=(*[jax.ShapeD...  3.63 us

profile of v3, /device:TPU:0, one launch (start us, length us, event | category | flops | bytes accessed | tf_op | source)
XLA Modules:
  0.0 122.3 jit_solution(13106281383312655239)
XLA Ops:
  1.3 117.2 %step.1 = (bf16[2,960,128]{2,1,0:T(8,128)(2,1)}, f32[8,256]{1,0:T(8,128)}) custom-call(bf16[602,256]{1,0:T(8,128)(2,1)} %bitcast.15, bf16[2048,1024]{1,0:T(8,128)(2,1)} %adj_ref.1, s32[4,4]{1,0:T(4,128)} %occ_ref.1, s32[1,256]{1,0:T(1,128)} %bitcast.19, s32[1,256]{1,0:T(1,128)} %bitcast.20, s32[1]{0:T(128)S(6)} %copy.32.cnt_ref, f32[602,256]{1,0:T(8,128)} %refs_0_.1, ...), custom_call_target="tpu_custom_call" | custom-call | flops 6442450944 | bytes 4194304 | tf_op jit(solution)/shard_map/step/pallas_call | solution.py:1084
  118.5 3.6 %update.1 = (f32[602,256]{1,0:T(8,128)}, f32[602,256]{1,0:T(8,128)}, f32[602,256]{1,0:T(8,128)}, f32[256,256]{1,0:T(8,128)}, f32[256,256]{1,0:T(8,128)}, /*index...) custom-call(bf16[2,960,128]{2,1,0:T(8,128)(2,1)} %get-tuple-element., ...), custom_call_target="tpu_custom_call" | custom-call | tf_op jit(solution)/shard_map/update/pallas_call | solution.py:1142

commit v4 on v3

--- a/solution.py
+++ b/solution.py
@@ -31,8 +31,8 @@
     second_new = B_TWO * second + (1.0 - B_TWO) * grad * grad
     fix_one = 1.0 - B_ONE**STEP
     fix_two = 1.0 - B_TWO**STEP
-    step_size = first_new / fix_one / (jnp.sqrt(second_new / fix_two) + EPSILON) + DECAY * weight
-    return (first_new, second_new, weight - RATE * step_size)
+    scaled = (first_new * (1.0 / fix_one)) / (jnp.sqrt(second_new * (1.0 / fix_two)) + EPSILON)
+    return (first_new, second_new, weight - RATE * (scaled + DECAY * weight))
 
 
 def up(value, unit):
@@ -337,8 +337,9 @@
                 sequence.append((3, q))
                 if q:
                     sequence.append((2, q - 1))
-            sequence += [(dz, q) for dz, q in ((2, nh - 1),)]
-            sequence += [(dz, q) for dz in (1, 0) for q in range(nh)]
+                sequence.append((1, q))
+            sequence.append((2, nh - 1))
+            sequence += [(0, q) for q in range(nh)]
         else:
             for q in range(nh):
                 sequence += [(dz, q) for dz in order if dz]
@@ -444,22 +445,28 @@
         act, slope = gelu_both(z2)
         acts[q] = act.astype(LOW) * valid_low[rows_q]
         slopes[q] = slope * valid_col[rows_q]
+        if (q + 1) % (nh // 2) == 0:
+            lane = q // (nh // 2)
+            some = jnp.concatenate(acts[lane * (nh // 2) : q + 1], axis=0)
+            y3t = dot_nt(w3t[...], some).astype(LOW)
+            mine = v3_half(c, lane)
+            mine[...] = y3t
+            for dy, dk in col_far:
+                send(mine, mine, gbase[0] + 2 * c + lane, (r, ys(dy) * nk + ks(dk)))
+
+    def v3_half(index, lane):
+        return v3_all.at[index, :, pl.ds(lane * (own // 2), own // 2)]
 
     spread(1, second_done)
     h2 = jnp.concatenate(acts, axis=0)
-    y3t = dot_nt(w3t[...], h2).astype(LOW)
 
     with jax.named_scope("hop3_gather"):
-        base = gbase[0]
-        mine = v3_all.at[c]
-        mine[...] = y3t
-        for dy, dk in col_far:
-            send(mine, mine, base + c, (r, ys(dy) * nk + ks(dk)))
         slope2t = jnp.concatenate(slopes, axis=0).T
         settle(s.n_col - 1)
-        for dy, dk in reversed(col_far):
-            source = ys(ny - dy) * nk + ks(nk - dk)
-            arrived(v3_all.at[source], base + source)
+        for lane in range(2):
+            for dy, dk in reversed(col_far):
+                source = ys(ny - dy) * nk + ks(nk - dk)
+                arrived(v3_half(source, lane), gbase[0] + 2 * source + lane)
     with jax.named_scope("hop3_sum"):
         pbase = wide[0]
         v3 = jnp.concatenate([v3_all[i] for i in range(s.n_col)], axis=1)
@@ -473,7 +480,7 @@
             place = dz * nx + dx
             arrived(p3recv.at[place], pbase + place)
             total = total + p3recv[place].astype(FULL)
-    total = total + y3t.astype(FULL)
+    total = total + v3_all[c].astype(FULL)
 
     place = lax.broadcasted_iota(jnp.int32, (s.cls, own), 0)
     real = place < s.classes
@@ -664,7 +671,7 @@
     with jax.named_scope("back2_rows"):
         settle()
         receive(0, lambda lane: dz2t[:, lane * half_own : (lane + 1) * half_own], features_out)
-    cbase = gbase[0] + s.n_col
+    cbase = gbase[0] + 2 * s.n_col
     ybase = gbase[1] + 2 * s.n_col
 
     def lane_part(index, lane):
@@ -843,24 +850,31 @@
                 source = ys(d) * nk + 1 - k
                 arrived(xt_all.at[source], xt_base + source)
 
-        def grad_one(index, start, stop):
+        low_core = (k == 0).astype(FULL)
+
+        def grad_one(start, stop):
             total = None
             end = min(stop, s.feat_up)
             for i in range(s.n_col):
-                here = acc[pl.ds(pl.multiple_of(index * lanes, lanes), lanes), :]
-                here = dot_nt(
-                    xt_all[i, start:end, :], here[:, i * own : (i + 1) * own].astype(LOW)
-                )
+                here = acc[:, i * own : (i + 1) * own].astype(LOW)
+                here = dot_nt(xt_all[i, start:end, :], here)
                 total = here if total is None else total + here
             if end < stop:
-                total = jnp.concatenate([total, jnp.zeros((stop - end, lanes), FULL)], axis=0)
-            return total
-
-        if nk > 1:
-            one_a.core_send(grad_one(1 - k, 0, s.cut_rows))
-            one_b.core_send(grad_one(1 - k, s.cut_rows, s.one_rows))
-        one_a.plane_send(grad_one(k, 0, s.cut_rows))
-        one_b.plane_send(grad_one(k, s.cut_rows, s.one_rows))
+                total = jnp.concatenate([total, jnp.zeros((stop - end, width), FULL)], axis=0)
+            if nk == 1:
+                return None, total
+            first, second = total[:, :lanes], total[:, lanes:]
+            return (
+                second * low_core + first * (1.0 - low_core),
+                first * low_core + second * (1.0 - low_core),
+            )
+
+        other, mine_a = grad_one(0, s.cut_rows)
+        one_a.core_send(other)
+        other, mine_b = grad_one(s.cut_rows, s.one_rows)
+        one_b.core_send(other)
+        one_a.plane_send(mine_a)
+        one_b.plane_send(mine_b)
         ones = jnp.ones((8, own), LOW)
         row = lax.broadcasted_iota(jnp.int32, (8, width), 0)
         lane = lax.broadcasted_iota(jnp.int32, (8, width), 1)
@@ -930,94 +944,53 @@
 
 
 def update_pieces(s):
-    middle = up(s.feat // 2, 8)
-    return (
-        (0, 0, middle),
-        (0, middle, s.feat - middle),
-        (1, 0, s.width),
-        (2, 0, s.classes),
-    )
-
-
-def adam_kernel(s, grad_hbm, misc_hbm, *refs):
+    some = up(s.feat // 4, 16)
+    cuts = [min(i * some, s.feat) for i in range(5)]
+    one = [(0, start, stop - start) for start, stop in zip(cuts, cuts[1:]) if stop > start]
+    return (*one, (1, 0, s.width), (2, 0, s.classes))
+
+
+def adam_kernel(s, grad_ref, misc_ref, *refs):
     ins, outs, scratch = refs[:12], refs[12:26], refs[26:]
-    grad_ref, misc_ref, bias_in, bias_out, ends, *held = scratch[:-2]
-    sem_in, sem_out = scratch[-2:]
-    pieces = update_pieces(s)
+    bias_out, ends, *held = scratch[:-1]
+    sem_out = scratch[-1]
     width, classes, lanes = s.width, s.classes, s.lanes
     grad_at = (0, s.one_rows, s.one_rows + width)
 
-    misc_load = pltpu.make_async_copy(misc_hbm.at[pl.ds(0, 8)], misc_ref, sem_in.at[0])
-    grad_load = pltpu.make_async_copy(
-        grad_hbm.at[:, pl.ds(0, s.grad_rows)], grad_ref, sem_in.at[1]
-    )
-    misc_load.start()
-    grad_load.start()
-    loads, count = [], 2
-    for n, (which, start, rows) in enumerate(pieces):
-        mine = []
-        for i in range(3):
-            mine.append(
-                pltpu.make_async_copy(
-                    ins[3 * which + i].at[pl.ds(start, rows)], held[2 * n].at[i], sem_in.at[count]
-                )
-            )
-            count += 1
-            mine[-1].start()
-        loads.append(mine)
-    bias_loads = []
-    for i in range(3):
-        bias_loads.append(
-            pltpu.make_async_copy(ins[9 + i], bias_in[i], sem_in.at[count])
-        )
-        count += 1
-        bias_loads[-1].start()
-
-    misc_load.wait()
-    grad_load.wait()
+    stores = []
+
+    def store(source, target):
+        copy = pltpu.make_async_copy(source, target, sem_out.at[len(stores)])
+        copy.start()
+        stores.append(copy)
+
     total = misc_ref[3:4, 1:2]
     scale = misc_ref[4:5, 0:1]
-    stores, count = [], 2
-    ends[0] = misc_ref[3:4, 0:1]
-    ends[1] = total
-    for i in range(2):
-        stores.append(pltpu.make_async_copy(ends.at[i], outs[12 + i], sem_out.at[i]))
-        stores[-1].start()
-    for n, (which, start, rows) in enumerate(pieces):
-        for load in loads[n]:
-            load.wait()
-        source, target = held[2 * n], held[2 * n + 1]
+    for (which, start, rows), target in zip(update_pieces(s), held):
+        span = slice(start, start + rows)
         for i in range(s.nk):
             lane = slice(i * lanes, (i + 1) * lanes)
             first = grad_at[which] + start
             grad = grad_ref[i, first : first + up(rows, 16), :].astype(FULL)[:rows]
-            weight, one, two = (source[j, :, lane] for j in range(3))
+            weight, one, two = (ins[3 * which + j][span, lane] for j in range(3))
             for j, new in enumerate(adam_update(weight, one, two, grad * scale)):
                 target[j, :, lane] = new
         for j in range(3):
-            stores.append(
-                pltpu.make_async_copy(
-                    target.at[j], outs[3 * which + j].at[pl.ds(start, rows)], sem_out.at[count]
-                )
-            )
-            count += 1
-            stores[-1].start()
-    for load in bias_loads:
-        load.wait()
+            store(target.at[j], outs[3 * which + j].at[pl.ds(start, rows)])
     for i, size in enumerate((width, width, classes)):
         span = slice(i * width, i * width + size)
-        weight, first, second = (bias_in[j][span] for j in range(3))
+        weight, first, second = (ins[9 + j][span] for j in range(3))
         new = adam_update(weight, first, second, misc_ref[i, :size] * misc_ref[4, :size])
         for j in range(3):
             bias_out[j][span] = new[j]
     for j in range(3):
-        stores.append(
-            pltpu.make_async_copy(bias_out[j], outs[9 + j], sem_out.at[count])
-        )
-        count += 1
-        stores[-1].start()
-    for store in stores:
-        store.wait()
+        store(bias_out[j], outs[9 + j])
+    ends[0] = misc_ref[3:4, 0:1]
+    ends[1] = total
+    for i in range(2):
+        store(ends.at[i], outs[12 + i])
+    for copy in stores:
+        copy.wait()
 
 
 def shards(
@@ -1080,12 +1053,12 @@
         ((s.nz, 8, width), FULL),
     ]
     bytes_held = sum(math.prod(shape) * jnp.dtype(kind).itemsize for shape, kind in shapes)
-    limit = 62 * 2**20
+    limit = min(62, 16 + bytes_held // 2**20) * 2**20
     grads, misc = pl.pallas_call(
         functools.partial(kernel, s),
         out_shape=(
-            jax.ShapeDtypeStruct((s.nk, s.grad_rows, lanes), LOW),
-            jax.ShapeDtypeStruct((8, width), FULL),
+            pltpu.VMEM((s.nk, s.grad_rows, lanes), LOW),
+            pltpu.VMEM((8, width), FULL),
         ),
         in_specs=[
             vmem,
@@ -1114,16 +1087,20 @@
         ),
         name="step",
     )(
-        features.T,
-        adjacency,
-        occupancy,
-        labels.reshape(1, own),
-        train_mask.reshape(1, own),
+        *[
+            pltpu.with_memory_space_constraint(a, pltpu.HBM)
+            for a in (features.T, adjacency)
+        ],
+        pltpu.with_memory_space_constraint(occupancy, pltpu.HBM),
+        *[
+            pltpu.with_memory_space_constraint(a, pltpu.HBM)
+            for a in (labels.reshape(1, own), train_mask.reshape(1, own))
+        ],
         node_count,
-        weight_one,
-        weight_two,
-        weight_three.T,
-        biases,
+        *[
+            pltpu.with_memory_space_constraint(a, pltpu.HBM)
+            for a in (weight_one, weight_two, weight_three.T, biases)
+        ],
     )
     state = (
         weight_one,
@@ -1146,23 +1123,15 @@
             jax.ShapeDtypeStruct((1, 1), FULL),
             jax.ShapeDtypeStruct((1, 1), FULL),
         ),
-        in_specs=[anywhere] * 14,
+        in_specs=[vmem] * 14,
         out_specs=(anywhere,) * 14,
         scratch_shapes=[
-            pltpu.VMEM((s.nk, s.grad_rows, lanes), LOW),
-            pltpu.VMEM((8, width), FULL),
-            [pltpu.VMEM(biases.shape, FULL)] * 3,
             [pltpu.VMEM(biases.shape, FULL)] * 3,
             pltpu.VMEM((2, 1, 1), FULL),
-            *[
-                pltpu.VMEM((3, rows, width), FULL)
-                for _, _, rows in update_pieces(s)
-                for _ in range(2)
-            ],
-            pltpu.SemaphoreType.DMA((17,)),
-            pltpu.SemaphoreType.DMA((17,)),
+            *[pltpu.VMEM((3, rows, width), FULL) for _, _, rows in update_pieces(s)],
+            pltpu.SemaphoreType.DMA((3 * len(update_pieces(s)) + 5,)),
         ],
-        compiler_params=pltpu.CompilerParams(vmem_limit_bytes=62 * 2**20),
+        compiler_params=pltpu.CompilerParams(vmem_limit_bytes=32 * 2**20),
         name="update",
     )(grads, misc, *state)
     return (

time: 123 us -> 121 us (0.984)
  Pallas kernels: 121 us -> 119 us
    pallas_call x1, Pallas kernels: 3.63 us -> 2.15 us  [shards(): pl.pallas_call(functools.partial(adam_kernel, s), out_shape=(*[jax.ShapeD...]
where the time goes in v4:
time: 121 us; the launch traced here: 120 us
  Pallas kernels  119 us (98%)
  between operations  1.66 us (1%)
    pallas_call x1, Pallas kernels, shards(): pl.pallas_call(functools.partial(kernel, s), out_shape=(pltpu.VMEM((s.nk,...  117 us

profile of v4, /device:TPU:0, one launch (start us, length us, event | category | flops | bytes accessed | tf_op | source)
XLA Modules:
  0.0 120.4 jit_solution(3151876336188413003)
XLA Ops:
  1.3 0.0 copy-start
  1.3 0.0 copy-start.1
  1.3 0.0 copy-start.2
  1.3 0.0 copy-start.3
  1.3 0.0 copy-start.4
  1.3 0.0 copy-start.5
  1.4 0.0 copy-start.6
  1.4 0.0 copy-start.7
  1.4 0.0 copy-start.8
  1.4 0.0 copy-start.9
  1.4 0.0 copy-start.10
  1.4 0.0 copy-start.11
  1.4 116.5 %step.1 = (bf16[2,960,128]{2,1,0:T(8,128)(2,1)S(1)}, f32[8,256]{1,0:T(8,128)S(1)}) custom-call(bf16[602,256]{1,0:T(8,128)(2,1)} %bitcast.15, bf16[2048,1024]{1,0:T(8,128)(2,1)} %adj_ref.1, s32[4,4]{1,0:T(4,128)} %occ_ref.1, s32[1,256]{1,0:T(1,128)} %bitcast.19, s32[1,256]{1,0:T(1,128)} %bitcast.20, s32[1]{0:T(128)S(6)} %copy.32.cnt_ref, f32[602,256]{1,0:T(8,128)} %refs_0_.1, ...), custom_call_target="tpu_custom_call" | custom-call | flops 6442450944 | bytes 4194304 | tf_op jit(solution)/shard_map/step/pallas_call | solution.py:1057
  118.0 0.0 copy-done
  118.0 0.0 copy-done.1
  118.0 0.0 copy-done.2
  118.0 0.0 copy-done.3
  118.0 0.0 copy-done.4
  118.0 0.0 copy-done.5
  118.0 0.0 copy-done.6
  118.0 0.0 copy-done.7
  118.0 0.0 copy-done.8
  118.1 0.0 copy-done.9
  118.1 2.2 %update.1 = (f32[602,256]{1,0:T(8,128)}, f32[602,256]{1,0:T(8,128)}, f32[602,256]{1,0:T(8,128)}, f32[256,256]{1,0:T(8,128)}, f32[256,256]{1,0:T(8,128)}, /*index...) custom-call(bf16[2,960,128]{2,1,0:T(8,128)(2,1)S(1)} %get-tuple-elem, ...), custom_call_target="tpu_custom_call" | custom-call | tf_op jit(solution)/shard_map/update/pallas_call | solution.py:1119
  (2 shorter events, 0.0 us)
Async XLA Ops:
  1.3 116.7 %copy-start = (f32[602,256]{1,0:T(8,128)S(1)}, f32[602,256]{1,0:T(8,128)}, u32[]{:S(2)}) copy-start(f32[602,256]{1,0:T(8,128)} %refs_0_.1) | copy-start | bytes 1849348
  1.3 116.7 %copy-start.1 = (f32[602,256]{1,0:T(8,128)S(1)}, f32[602,256]{1,0:T(8,128)}, u32[]{:S(2)}) copy-start(f32[602,256]{1,0:T(8,128)} %refs_1_.1) | copy-start | bytes 1849348
  1.3 116.7 %copy-start.2 = (f32[602,256]{1,0:T(8,128)S(1)}, f32[602,256]{1,0:T(8,128)}, u32[]{:S(2)}) copy-start(f32[602,256]{1,0:T(8,128)} %refs_2_.1) | copy-start | bytes 1849348
  1.3 116.7 %copy-start.3 = (f32[256,256]{1,0:T(8,128)S(1)}, f32[256,256]{1,0:T(8,128)}, u32[]{:S(2)}) copy-start(f32[256,256]{1,0:T(8,128)} %refs_3_.1) | copy-start | bytes 786436
  1.3 116.7 %copy-start.4 = (f32[256,256]{1,0:T(8,128)S(1)}, f32[256,256]{1,0:T(8,128)}, u32[]{:S(2)}) copy-start(f32[256,256]{1,0:T(8,128)} %refs_4_.1) | copy-start | bytes 786436
  1.3 116.7 %copy-start.5 = (f32[256,256]{1,0:T(8,128)S(1)}, f32[256,256]{1,0:T(8,128)}, u32[]{:S(2)}) copy-start(f32[256,256]{1,0:T(8,128)} %refs_5_.1) | copy-start | bytes 786436
  1.4 116.7 %copy-start.6 = (f32[256,41]{0,1:T(8,128)S(1)}, f32[256,41]{0,1:T(8,128)}, u32[]{:S(2)}) copy-start(f32[256,41]{0,1:T(8,128)} %param.26) | copy-start | bytes 125956
  1.4 116.7 %copy-start.7 = (f32[256,41]{0,1:T(8,128)S(1)}, f32[256,41]{0,1:T(8,128)}, u32[]{:S(2)}) copy-start(f32[256,41]{0,1:T(8,128)} %param.30) | copy-start | bytes 125956
  1.4 116.7 %copy-start.8 = (f32[256,41]{0,1:T(8,128)S(1)}, f32[256,41]{0,1:T(8,128)}, u32[]{:S(2)}) copy-start(f32[256,41]{0,1:T(8,128)} %param.34) | copy-start | bytes 125956
  1.4 116.7 %copy-start.9 = (f32[553]{0:T(1024)S(1)}, f32[553]{0:T(1024)}, u32[]{:S(2)}) copy-start(f32[553]{0:T(1024)} %refs_9_.1) | copy-start | bytes 6640
  1.4 116.7 %copy-start.10 = (f32[553]{0:T(1024)S(1)}, f32[553]{0:T(1024)}, u32[]{:S(2)}) copy-start(f32[553]{0:T(1024)} %refs_10_.1) | copy-start | bytes 6640
  1.4 116.7 %copy-start.11 = (f32[553]{0:T(1024)S(1)}, f32[553]{0:T(1024)}, u32[]{:S(2)}) copy-start(f32[553]{0:T(1024)} %refs_11_.1) | copy-start | bytes 6640

commit v5 on v4

--- a/solution.py
+++ b/solution.py
@@ -65,13 +65,15 @@
         self.feat_up = up(feat, 128)
         self.cls = up(classes, 16)
         self.plane = self.nx * self.ny
-        self.one_rows = up(feat, 16 * self.plane)
+        self.one_rows = up(feat + 1, 16 * self.plane)
         self.two_rows = up(width + self.cls, 16 * self.plane)
         self.grad_rows = self.one_rows + self.two_rows
         self.lanes = width // self.nk
         units = self.one_rows // (16 * self.plane)
         self.cut_rows = (units + 1) // 2 * 16 * self.plane
-        self.nh = 4
+        cuts = [own // 4 * i for i in range(5)]
+        self.parts = [(start, stop - start) for start, stop in zip(cuts, cuts[1:])]
+        self.nh = len(self.parts)
         self.relayed = self.nz == 4
         self.sends = 3 * (n_row + n_col) + 3 * self.plane
         wide = 2 * self.nh * (n_row + n_col)
@@ -238,13 +240,17 @@
         return pl.ds(pl.multiple_of(index * own, own), own)
 
     nh = s.nh
-    cut = own // nh
 
     def row_part(index, q):
-        return pl.ds(pl.multiple_of(index * own + q * cut, cut), cut)
+        start, count = s.parts[q]
+        return pl.ds(pl.multiple_of(index * own + start, count), count)
 
     def part(q):
-        return pl.ds(q * cut, cut)
+        return pl.ds(*s.parts[q])
+
+    def span_of(q):
+        start, count = s.parts[q]
+        return slice(start, start + count)
 
     valid_col = (lax.broadcasted_iota(jnp.int32, (own, width), 0) < cnt_ref[0]).astype(FULL)
     valid_low = valid_col.astype(LOW)
@@ -295,7 +301,7 @@
     with jax.named_scope("barrier"):
         pl.semaphore_wait(barrier, len(peers))
     for q in range(nh):
-        start_gather(0, q, y1[q * cut : (q + 1) * cut])
+        start_gather(0, q, y1[span_of(q)])
 
     if relayed:
 
@@ -363,7 +369,7 @@
                 )
 
         def send_z(dz, q):
-            rows_q = slice(q * cut, (q + 1) * cut)
+            rows_q = span_of(q)
             total = acc[rows_q, dz * own : (dz + 1) * own]
             for dx in range(1, nx):
                 place = (dx - 1) * nz + dz
@@ -402,7 +408,7 @@
 
         def sum_z(q):
             total = totals[q]
-            rows_q = slice(q * cut, (q + 1) * cut)
+            rows_q = span_of(q)
             for dz in range(1, nz):
                 there, mark = zrecv.at[hop, dz - 1, part(q)], zbase + dz * nh + q
                 if relayed and dz == 3:
@@ -426,7 +432,7 @@
     slopes, acts = [None] * nh, [None] * nh
 
     def first_done(q, total):
-        rows_q = slice(q * cut, (q + 1) * cut)
+        rows_q = span_of(q)
         z1 = total + v_all[0, row_part(c, q), :].astype(FULL) + bias[0]
         act, slope = gelu_both(z1)
         h1 = act.astype(LOW) * valid_low[rows_q]
@@ -440,14 +446,16 @@
     xt_base = gbase[1] + s.n_col
 
     def second_done(q, total):
-        rows_q = slice(q * cut, (q + 1) * cut)
+        rows_q = span_of(q)
         z2 = total + v_all[1, row_part(c, q), :].astype(FULL) + bias[1]
         act, slope = gelu_both(z2)
         acts[q] = act.astype(LOW) * valid_low[rows_q]
         slopes[q] = slope * valid_col[rows_q]
-        if (q + 1) % (nh // 2) == 0:
-            lane = q // (nh // 2)
-            some = jnp.concatenate(acts[lane * (nh // 2) : q + 1], axis=0)
+        ends = span_of(q).stop
+        if ends % (own // 2) == 0:
+            lane = 2 * ends // own - 1
+            some = [act for i, act in enumerate(acts[: q + 1]) if span_of(i).start >= ends - own // 2]
+            some = jnp.concatenate(some, axis=0)
             y3t = dot_nt(w3t[...], some).astype(LOW)
             mine = v3_half(c, lane)
             mine[...] = y3t
@@ -548,7 +556,7 @@
 
     quarters = [(lane, row) for lane in range(2) for row in range(2)]
     def receive(hop, values, meanwhile=None, late=None):
-        base = wide[hop]
+        base, np = wide[hop], len(quarters)
         first = hop * s.n_row
 
         def piece(dz, dx, q):
@@ -558,7 +566,7 @@
             return send(
                 piece(0, 0, q),
                 piece(dz, 0, q),
-                base + dz * nh + q,
+                base + dz * np + q,
                 at(zs(dz), x, y, k),
                 when=when,
                 start=start,
@@ -569,7 +577,7 @@
                 send(
                     piece(dz, 0, q),
                     piece(dz, dx, q),
-                    base + (dx * nz + dz) * nh + q,
+                    base + (dx * nz + dz) * np + q,
                     at(z, xs(dx), y, k),
                     start=start,
                 )
@@ -598,11 +606,11 @@
             meanwhile()
 
         passing = {
-            (dz, q): to_x(dz, q, start=False) for q in range(nh) for dz in range(1, nz)
+            (dz, q): to_x(dz, q, start=False) for q in range(np) for dz in range(1, nz)
         }
 
         def step(dz, q):
-            arrived(piece(dz, 0, q), base + dz * nh + q)
+            arrived(piece(dz, 0, q), base + dz * np + q)
             for copy in passing[dz, q]:
                 copy.start()
 
@@ -611,19 +619,19 @@
                 send(
                     piece(2, 0, q),
                     piece(3, 0, q),
-                    base + 3 * nh + q,
+                    base + 3 * np + q,
                     at(zs(1), x, y, k),
                     when=inner,
                     start=False,
                 )
-                for q in range(nh)
+                for q in range(np)
             ]
-            paced = [to_z(3, q, inner, start=False) for q in range(nh)]
+            paced = [to_z(3, q, inner, start=False) for q in range(np)]
 
             @pl.when(inner)
             def _():
-                for q in range(nh):
-                    arrived(piece(2, 0, q), base + 2 * nh + q)
+                for q in range(np):
+                    arrived(piece(2, 0, q), base + 2 * np + q)
                     relays[q].start()
                     paced[q].start()
                     for copy in passing[2, q]:
@@ -631,22 +639,22 @@
                     step(1, q)
                     if q > 1:
                         step(3, q - 2)
-                for q in range(nh - 2, nh):
+                for q in range(np - 2, np):
                     step(3, q)
 
             @pl.when(outer)
             def _():
-                for q in range(nh + 2):
-                    if q < nh:
+                for q in range(np + 2):
+                    if q < np:
                         step(1, q)
-                    if 0 < q <= nh:
+                    if 0 < q <= np:
                         step(2, q - 1)
                     if q > 2:
                         step(3, q - 3)
-                for q in range(nh - 1, nh):
+                for q in range(np - 1, np):
                     step(3, q)
         else:
-            for q in range(nh):
+            for q in range(np):
                 for dz in range(1, nz):
                     step(dz, q)
         for dz in range(1, nz):
@@ -655,8 +663,8 @@
             late()
         for dz in range(nz):
             for dx in range(1, nx):
-                for q in range(nh):
-                    arrived(piece(dz, dx, q), base + (dx * nz + dz) * nh + q)
+                for q in range(np):
+                    arrived(piece(dz, dx, q), base + (dx * nz + dz) * np + q)
                 gained(pool[first + dx * nz + dz], source(dz, dx))
 
     dz2t = (dh2t * slope2t).astype(LOW)
@@ -810,22 +818,29 @@
                 for i in range(plane):
                     arrived(fin.at[1 - k, self.piece(i)], base + plane + i)
 
-    written = []
-
     def write(start, count):
-        rows_w = pl.ds(start, count)
-        copy = pltpu.make_async_copy(
-            fin.at[:, rows_w], grad_ref.at[:, rows_w], lsem.at[n_sub + len(written)]
-        )
-        copy.start()
-        written.append(copy)
+        grad_ref[:, start : start + count, :] = fin[:, start : start + count, :]
 
     one_a = Total(0, s.cut_rows)
     one_b = Total(s.cut_rows, s.one_rows - s.cut_rows)
     two = Total(s.one_rows, s.two_rows)
     tail = s.two_rows - width - s.cls
 
+    ones = jnp.ones((8, own), LOW)
+    row = lax.broadcasted_iota(jnp.int32, (8, width), 0)
+    lane_of = lax.broadcasted_iota(jnp.int32, (8, width), 1)
+    bias_three = jnp.concatenate([dlt, jnp.zeros((width - s.cls, own), LOW)], axis=0)
+    misc = jnp.where(row == 1, dot_nt(ones, dz2t), 0.0)
+    misc = jnp.where(row == 2, dot_nt(ones, bias_three), misc)
+    misc = jnp.where((row == 3) & (lane_of == 0), loss, misc)
+    misc = jnp.where((row == 3) & (lane_of == 1), number, misc)
+    mbase = rslots(1 + plane + nz)
+    plane_base, line_base = mbase + 1, mbase + 1 + plane
+
     def early():
+        misc_k[0] = misc
+        if nk > 1:
+            send(misc_k.at[0], misc_k.at[1], mbase, sibling)
         grad3t = dot(qt, h2)
         dy2t = jnp.concatenate(dy2_parts, axis=1)
         grad2 = dot_nt(h1t, dy2t)
@@ -839,9 +854,28 @@
             two.plane_send(first * low_core + second * (1.0 - low_core))
         else:
             two.plane_send(acc_two)
+        here = misc_k[0]
+        if nk > 1:
+            arrived(misc_k.at[1], mbase)
+            here = here + misc_k[1]
+        misc_p[me] = here
+        for dx, dy in others:
+            send(misc_p.at[me], misc_p.at[me], plane_base + me, at(z, xs(dx), ys(dy), k))
+
+    def late():
+        two.line_send()
+        for dx, dy in others:
+            there = ys(dy) * nx + xs(dx)
+            arrived(misc_p.at[there], plane_base + there)
+        here = misc_p[0]
+        for i in range(1, plane):
+            here = here + misc_p[i]
+        misc_z[z] = here
+        for dz in range(1, nz):
+            send(misc_z.at[z], misc_z.at[z], line_base + z, at(zs(dz), x, y, k))
 
     with jax.named_scope("back1_rows"):
-        receive(1, first_slopes, early, two.line_send)
+        receive(1, first_slopes, early, late)
     with jax.named_scope("grad1"):
         dz1t = jnp.concatenate(dz1_parts, axis=1)
         acc[:, row_block(c)] += dz1t.astype(FULL)
@@ -851,6 +885,7 @@
                 arrived(xt_all.at[source], xt_base + source)
 
         low_core = (k == 0).astype(FULL)
+        bias_one = dot_nt(ones, dz1t)[0:1, :]
 
         def grad_one(start, stop):
             total = None
@@ -861,6 +896,10 @@
                 total = here if total is None else total + here
             if end < stop:
                 total = jnp.concatenate([total, jnp.zeros((stop - end, width), FULL)], axis=0)
+            bias_at = s.feat - start
+            if 0 <= bias_at < stop - start:
+                places = lax.broadcasted_iota(jnp.int32, (stop - start, width), 0)
+                total = jnp.where(places == bias_at, bias_one, total)
             if nk == 1:
                 return None, total
             first, second = total[:, :lanes], total[:, lanes:]
@@ -875,71 +914,35 @@
         one_b.core_send(other)
         one_a.plane_send(mine_a)
         one_b.plane_send(mine_b)
-        ones = jnp.ones((8, own), LOW)
-        row = lax.broadcasted_iota(jnp.int32, (8, width), 0)
-        lane = lax.broadcasted_iota(jnp.int32, (8, width), 1)
-        bias_three = jnp.concatenate([dlt, jnp.zeros((width - s.cls, own), LOW)], axis=0)
-        misc = jnp.where(row == 0, dot_nt(ones, dz1t), 0.0)
-        misc = jnp.where(row == 1, dot_nt(ones, dz2t), misc)
-        misc = jnp.where(row == 2, dot_nt(ones, bias_three), misc)
-        misc = jnp.where((row == 3) & (lane == 0), loss, misc)
-        misc = jnp.where((row == 3) & (lane == 1), number, misc)
-        mbase = rslots(1 + plane + nz)
-        misc_k[0] = misc
-        if nk > 1:
-            send(misc_k.at[0], misc_k.at[1], mbase, sibling)
 
     with jax.named_scope("sum_plane"):
-        if nk > 1:
-            arrived(misc_k.at[1], mbase)
-            misc = misc_k[0] + misc_k[1]
-        misc_p[me] = misc
-        mbase = mbase + 1
-        for dx, dy in others:
-            send(misc_p.at[me], misc_p.at[me], mbase + me, at(z, xs(dx), ys(dy), k))
         left = len(pending)
         two.back_send()
     with jax.named_scope("sum_line"):
         one_a.line_send()
         one_b.line_send()
-        for dx, dy in others:
-            there = ys(dy) * nx + xs(dx)
-            arrived(misc_p.at[there], mbase + there)
-        misc = misc_p[0]
-        for i in range(1, plane):
-            misc = misc + misc_p[i]
-        mbase = mbase + plane
-        misc_z[z] = misc
-        for dz in range(1, nz):
-            send(misc_z.at[z], misc_z.at[z], mbase + z, at(zs(dz), x, y, k))
-        two.back_forward()
-        two.end()
-        settle(len(pending) - left)
     with jax.named_scope("back_line"):
         one_a.back_send()
         one_b.back_send()
         for dz in range(1, nz):
-            arrived(misc_z.at[zback(dz)], mbase + zback(dz))
+            arrived(misc_z.at[zback(dz)], line_base + zback(dz))
         misc = misc_z[0]
         for i in range(1, nz):
             misc = misc + misc_z[i]
-        misc_k[0] = jnp.where(row == 4, 1.0 / misc[3:4, 1:2], misc)
-        written.append(
-            pltpu.make_async_copy(misc_k.at[0], misc_ref.at[pl.ds(0, 8)], lsem.at[n_sub])
-        )
-        written[0].start()
-        write(s.one_rows, s.two_rows)
+        misc_ref[...] = jnp.where(row == 4, 1.0 / misc[3:4, 1:2], misc)
+        settle(len(pending) - left)
     with jax.named_scope("back_plane"):
         one_a.back_forward()
         one_b.back_forward()
+        two.back_forward()
         one_a.end()
         write(0, s.cut_rows)
         one_b.end()
         write(s.cut_rows, s.one_rows - s.cut_rows)
+        two.end()
+        write(s.one_rows, s.two_rows)
     with jax.named_scope("settle"):
         settle()
-        for copy in written:
-            copy.wait()
     assert rcount[0] <= s.arrivals
 
 
@@ -980,7 +983,12 @@
     for i, size in enumerate((width, width, classes)):
         span = slice(i * width, i * width + size)
         weight, first, second = (ins[9 + j][span] for j in range(3))
-        new = adam_update(weight, first, second, misc_ref[i, :size] * misc_ref[4, :size])
+        grad = misc_ref[i, :size]
+        if not i:
+            top = s.feat // 16 * 16
+            rows = [grad_ref[j, top : top + 16, :].astype(FULL) for j in range(s.nk)]
+            grad = jnp.concatenate([a[s.feat - top] for a in rows])
+        new = adam_update(weight, first, second, grad * misc_ref[4, :size])
         for j in range(3):
             bias_out[j][span] = new[j]
     for j in range(3):
@@ -1072,12 +1080,12 @@
             vmem,
             vmem,
         ],
-        out_specs=(anywhere, anywhere),
+        out_specs=(vmem, vmem),
         scratch_shapes=[
             *[pltpu.VMEM(shape, kind) for shape, kind in shapes],
             pltpu.SemaphoreType.DMA((s.sends,)),
             pltpu.SemaphoreType.DMA((s.arrivals,)),
-            pltpu.SemaphoreType.DMA((rows // SUB + 4,)),
+            pltpu.SemaphoreType.DMA((rows // SUB,)),
         ],
         compiler_params=pltpu.CompilerParams(
             collective_id=0, has_side_effects=True, vmem_limit_bytes=limit

time: 121 us -> 120 us (level)
  no operation moved by 1% of the time
where the time goes in v5:
time: 120 us
  Pallas kernels  118 us (98%)
  between operations  1.66 us (1%)
    pallas_call x1, Pallas kernels, shards(): pl.pallas_call(functools.partial(kernel, s), out_shape=(pltpu.VMEM((s.nk,...  116 us

profile of v5, /device:TPU:0, one launch (start us, length us, event | category | flops | bytes accessed | tf_op | source)
XLA Modules:
  0.0 120.1 jit_solution(345373748809777286)
XLA Ops:
  1.3 0.0 copy-start
  1.3 0.0 copy-start.1
  1.3 0.0 copy-start.2
  1.3 0.0 copy-start.3
  1.3 0.0 copy-start.4
  1.3 0.0 copy-start.5
  1.4 0.0 copy-start.6
  1.4 0.0 copy-start.7
  1.4 0.0 copy-start.8
  1.4 0.0 copy-start.9
  1.4 116.2 %step.1 = (bf16[2,960,128]{2,1,0:T(8,128)(2,1)S(1)}, f32[8,256]{1,0:T(8,128)S(1)}) custom-call(bf16[602,256]{1,0:T(8,128)(2,1)} %bitcast.15, bf16[2048,1024]{1,0:T(8,128)(2,1)} %adj_ref.1, s32[4,4]{1,0:T(4,128)} %occ_ref.1, s32[1,256]{1,0:T(1,128)} %bitcast.19, s32[1,256]{1,0:T(1,128)} %bitcast.20, s32[1]{0:T(128)S(6)} %copy.32.cnt_ref, f32[602,256]{1,0:T(8,128)} %refs_0_.1, ...), custom_call_target="tpu_custom_call" | custom-call | flops 6442450944 | bytes 4194304 | tf_op jit(solution)/shard_map/step/pallas_call | solution.py:1065
  117.6 0.0 copy-done
  117.6 0.0 copy-done.1
  117.6 0.0 copy-done.2
  117.7 0.0 copy-done.3
  117.7 0.0 copy-done.4
  117.7 0.0 copy-done.5
  117.7 0.0 copy-done.6
  117.7 0.0 copy-done.7
  117.7 0.0 copy-done.8
  117.7 0.0 copy-done.9
  117.7 0.0 copy-done.10
  117.7 0.0 copy-done.11
  117.7 2.2 %update.1 = (f32[602,256]{1,0:T(8,128)}, f32[602,256]{1,0:T(8,128)}, f32[602,256]{1,0:T(8,128)}, f32[256,256]{1,0:T(8,128)}, f32[256,256]{1,0:T(8,128)}, /*index...) custom-call(bf16[2,960,128]{2,1,0:T(8,128)(2,1)S(1)} %get-tuple-elem, ...), custom_call_target="tpu_custom_call" | custom-call | tf_op jit(solution)/shard_map/update/pallas_call | solution.py:1127
  (2 shorter events, 0.0 us)
Async XLA Ops:
  1.3 116.3 %copy-start = (f32[602,256]{1,0:T(8,128)S(1)}, f32[602,256]{1,0:T(8,128)}, u32[]{:S(2)}) copy-start(f32[602,256]{1,0:T(8,128)} %refs_0_.1) | copy-start | bytes 1849348
  1.3 116.3 %copy-start.1 = (f32[602,256]{1,0:T(8,128)S(1)}, f32[602,256]{1,0:T(8,128)}, u32[]{:S(2)}) copy-start(f32[602,256]{1,0:T(8,128)} %refs_1_.1) | copy-start | bytes 1849348
  1.3 116.3 %copy-start.2 = (f32[602,256]{1,0:T(8,128)S(1)}, f32[602,256]{1,0:T(8,128)}, u32[]{:S(2)}) copy-start(f32[602,256]{1,0:T(8,128)} %refs_2_.1) | copy-start | bytes 1849348
  1.3 116.3 %copy-start.3 = (f32[256,256]{1,0:T(8,128)S(1)}, f32[256,256]{1,0:T(8,128)}, u32[]{:S(2)}) copy-start(f32[256,256]{1,0:T(8,128)} %refs_3_.1) | copy-start | bytes 786436
  1.3 116.3 %copy-start.4 = (f32[256,256]{1,0:T(8,128)S(1)}, f32[256,256]{1,0:T(8,128)}, u32[]{:S(2)}) copy-start(f32[256,256]{1,0:T(8,128)} %refs_4_.1) | copy-start | bytes 786436
  1.3 116.3 %copy-start.5 = (f32[256,256]{1,0:T(8,128)S(1)}, f32[256,256]{1,0:T(8,128)}, u32[]{:S(2)}) copy-start(f32[256,256]{1,0:T(8,128)} %refs_5_.1) | copy-start | bytes 786436
  1.4 116.3 %copy-start.6 = (f32[256,41]{0,1:T(8,128)S(1)}, f32[256,41]{0,1:T(8,128)}, u32[]{:S(2)}) copy-start(f32[256,41]{0,1:T(8,128)} %param.26) | copy-start | bytes 125956
  1.4 116.3 %copy-start.7 = (f32[256,41]{0,1:T(8,128)S(1)}, f32[256,41]{0,1:T(8,128)}, u32[]{:S(2)}) copy-start(f32[256,41]{0,1:T(8,128)} %param.30) | copy-start | bytes 125956
  1.4 116.3 %copy-start.8 = (f32[256,41]{0,1:T(8,128)S(1)}, f32[256,41]{0,1:T(8,128)}, u32[]{:S(2)}) copy-start(f32[256,41]{0,1:T(8,128)} %param.34) | copy-start | bytes 125956
  1.4 116.3 %copy-start.9 = (f32[553]{0:T(1024)S(1)}, f32[553]{0:T(1024)}, u32[]{:S(2)}) copy-start(f32[553]{0:T(1024)} %refs_9_.1) | copy-start | bytes 6640
  1.4 116.3 %copy-start.10 = (f32[553]{0:T(1024)S(1)}, f32[553]{0:T(1024)}, u32[]{:S(2)}) copy-start(f32[553]{0:T(1024)} %refs_10_.1) | copy-start | bytes 6640
  1.4 116.3 %copy-start.11 = (f32[553]{0:T(1024)S(1)}, f32[553]{0:T(1024)}, u32[]{:S(2)}) copy-start(f32[553]{0:T(1024)} %refs_11_.1) | copy-start | bytes 6640

commit v6 on v5

--- a/solution.py
+++ b/solution.py
@@ -70,14 +70,16 @@
         self.grad_rows = self.one_rows + self.two_rows
         self.lanes = width // self.nk
         units = self.one_rows // (16 * self.plane)
-        self.cut_rows = (units + 1) // 2 * 16 * self.plane
+        chunks = min(3, units)
+        cuts = [units * i // chunks * 16 * self.plane for i in range(chunks + 1)]
+        self.chunks = list(zip(cuts, cuts[1:]))
         cuts = [own // 4 * i for i in range(5)]
         self.parts = [(start, stop - start) for start, stop in zip(cuts, cuts[1:])]
         self.nh = len(self.parts)
         self.relayed = self.nz == 4
         self.sends = 3 * (n_row + n_col) + 3 * self.plane
         wide = 2 * self.nh * (n_row + n_col)
-        self.arrivals = wide + 3 * (1 + 3 * self.plane + self.nz) + 1 + self.plane + self.nz
+        self.arrivals = wide + max(1, chunks - 1) * (1 + 3 * self.plane + self.nz) + 1 + self.plane + self.nz
 
 
 def kernel(
@@ -269,6 +271,7 @@
     y1 = lax.dot_general(
         own_xt[...], w1b[...], (((0,), (0,)), ((), ())), preferred_element_type=FULL
     ).astype(LOW)
+    v_all[0, row_block(c), :] = y1
 
     wide = [rslots(s.n_row * nh) for _ in range(2)]
     gbase = [rslots(s.n_col * nh) for _ in range(2)]
@@ -276,7 +279,8 @@
 
     def start_gather(hop, q, values):
         mine = v_all.at[hop, row_part(c, q)]
-        mine[...] = values
+        if values is not None:
+            mine[...] = values
         for d in range(1, ny):
             send(mine, mine, gbase[hop] + c * nh + q, at(z, x, ys(d), k))
         if nk > 1:
@@ -301,7 +305,7 @@
     with jax.named_scope("barrier"):
         pl.semaphore_wait(barrier, len(peers))
     for q in range(nh):
-        start_gather(0, q, y1[span_of(q)])
+        start_gather(0, q, None)
 
     if relayed:
 
@@ -339,13 +343,7 @@
 
         sequence = []
         if relayed:
-            for q in range(nh):
-                sequence.append((3, q))
-                if q:
-                    sequence.append((2, q - 1))
-                sequence.append((1, q))
-            sequence.append((2, nh - 1))
-            sequence += [(0, q) for q in range(nh)]
+            sequence = [(3, 0), (3, 1), (2, 0), (3, 2), (2, 1), (3, 3), (1, 0), (2, 2), (1, 1), (2, 3), (1, 2), (1, 3), (0, 0), (0, 1), (0, 2), (0, 3)]
         else:
             for q in range(nh):
                 sequence += [(dz, q) for dz in order if dz]
@@ -743,12 +741,13 @@
         return pl.ds(pl.multiple_of(index * lanes, lanes), lanes)
 
     class Total:
-        def __init__(self, start, rows):
+        def __init__(self, start, rows, mark=None, base=None):
             self.all = pl.ds(start, rows)
             self.start, self.rows = start, rows
             self.n = rows // plane
             self.short = pl.ds(start // plane, self.n)
-            self.base = rslots(1 + 3 * plane + nz)
+            self.mark = rslots(1) if mark is None else mark
+            self.base = rslots(3 * plane + nz) if base is None else base
 
         def piece(self, index):
             return pl.ds(pl.multiple_of(self.start + index * self.n, 16), self.n)
@@ -756,14 +755,14 @@
         def core_send(self, other):
             if nk > 1:
                 half_send[self.all, :] = other.astype(LOW)
-                send(half_send.at[self.all], half_recv.at[self.all], self.base, sibling)
+                send(half_send.at[self.all], half_recv.at[self.all], self.mark, sibling)
 
         def plane_send(self, mine):
             if nk > 1:
-                arrived(half_recv.at[self.all], self.base)
+                arrived(half_recv.at[self.all], self.mark)
                 mine = mine + half_recv[self.all, :].astype(FULL)
             half[self.all, :] = mine.astype(LOW)
-            base = self.base + 1
+            base = self.base
             for dx, dy in others:
                 there = ys(dy) * nx + xs(dx)
                 send(
@@ -775,7 +774,7 @@
             plane_recv[me, self.short, :] = half[self.piece(me), :]
 
         def line_send(self):
-            base = self.base + 1
+            base = self.base
             for dx, dy in others:
                 there = ys(dy) * nx + xs(dx)
                 arrived(plane_recv.at[there, self.short], base + there)
@@ -784,18 +783,18 @@
                 total = total + plane_recv[i, self.short, :].astype(FULL)
             quarter[z, self.short, :] = total.astype(LOW)
             mine = quarter.at[z, self.short]
-            base = self.base + 1 + plane
+            base = self.base + plane
             for dz in range(nz - 1, 0, -1):
                 send(mine, mine, base + z, at(zs(dz), x, y, k))
 
         def back_send(self):
-            base = self.base + 1 + plane
+            base = self.base + plane
             for dz in range(1, nz):
                 arrived(quarter.at[zback(dz), self.short], base + zback(dz))
             total = quarter[0, self.short, :].astype(FULL)
             for i in range(1, nz):
                 total = total + quarter[i, self.short, :].astype(FULL)
-            base = self.base + 1 + plane + nz
+            base = self.base + plane + nz
             mine = fin.at[k, self.piece(me)]
             mine[...] = total.astype(LOW)
             for dx, dy in others:
@@ -804,7 +803,7 @@
                 send(mine, mine, base + plane + me, sibling)
 
         def back_forward(self):
-            base = self.base + 1 + plane + nz
+            base = self.base + plane + nz
             for dx, dy in others:
                 there = ys(dy) * nx + xs(dx)
                 block = fin.at[k, self.piece(there)]
@@ -813,7 +812,7 @@
                     send(block, block, base + plane + there, sibling)
 
         def end(self):
-            base = self.base + 1 + plane + nz
+            base = self.base + plane + nz
             if nk > 1:
                 for i in range(plane):
                     arrived(fin.at[1 - k, self.piece(i)], base + plane + i)
@@ -821,8 +820,14 @@
     def write(start, count):
         grad_ref[:, start : start + count, :] = fin[:, start : start + count, :]
 
-    one_a = Total(0, s.cut_rows)
-    one_b = Total(s.cut_rows, s.one_rows - s.cut_rows)
+    ones_at = [
+        (gbase[i] + 2 * s.n_col + 2 * ny, wide[0] + i * (3 * plane + nz)) for i in range(2)
+    ]
+    ones_at += [(None, None)] * len(s.chunks)
+    assert 2 * (3 * plane + nz) <= s.n_row * nh
+    one = [
+        Total(start, stop - start, *there) for (start, stop), there in zip(s.chunks, ones_at)
+    ]
     two = Total(s.one_rows, s.two_rows)
     tail = s.two_rows - width - s.cls
 
@@ -908,22 +913,24 @@
                 first * low_core + second * (1.0 - low_core),
             )
 
-        other, mine_a = grad_one(0, s.cut_rows)
-        one_a.core_send(other)
-        other, mine_b = grad_one(s.cut_rows, s.one_rows)
-        one_b.core_send(other)
-        one_a.plane_send(mine_a)
-        one_b.plane_send(mine_b)
+        waiting = None
+        for chunk, (start, stop) in zip(one, s.chunks):
+            other, mine = grad_one(start, stop)
+            chunk.core_send(other)
+            if waiting is not None:
+                waiting()
+            waiting = functools.partial(chunk.plane_send, mine)
+        waiting()
 
     with jax.named_scope("sum_plane"):
         left = len(pending)
         two.back_send()
     with jax.named_scope("sum_line"):
-        one_a.line_send()
-        one_b.line_send()
+        for chunk in one:
+            chunk.line_send()
     with jax.named_scope("back_line"):
-        one_a.back_send()
-        one_b.back_send()
+        for chunk in one:
+            chunk.back_send()
         for dz in range(1, nz):
             arrived(misc_z.at[zback(dz)], line_base + zback(dz))
         misc = misc_z[0]
@@ -932,13 +939,12 @@
         misc_ref[...] = jnp.where(row == 4, 1.0 / misc[3:4, 1:2], misc)
         settle(len(pending) - left)
     with jax.named_scope("back_plane"):
-        one_a.back_forward()
-        one_b.back_forward()
+        for chunk in one:
+            chunk.back_forward()
         two.back_forward()
-        one_a.end()
-        write(0, s.cut_rows)
-        one_b.end()
-        write(s.cut_rows, s.one_rows - s.cut_rows)
+        for chunk in one:
+            chunk.end()
+            write(chunk.start, chunk.rows)
         two.end()
         write(s.one_rows, s.two_rows)
     with jax.named_scope("settle"):

time: 120 us -> 119 us (level)
    pallas_call x1, Pallas kernels: 116 us -> 115 us  [shards(): pl.pallas_call(functools.partial(kernel, s), out_shape=(pltpu.VMEM((s.nk,...]
where the time goes in v6:
time: 119 us
  Pallas kernels  117 us (98%)
  between operations  1.66 us (1%)
    pallas_call x1, Pallas kernels, shards(): pl.pallas_call(functools.partial(kernel, s), out_shape=(pltpu.VMEM((s.nk,...  115 us

profile of v6, /device:TPU:0, one launch (start us, length us, event | category | flops | bytes accessed | tf_op | source)
XLA Modules:
  0.0 118.8 jit_solution(14713521568490354573)
XLA Ops:
  1.3 0.0 copy-start
  1.3 0.0 copy-start.1
  1.3 0.0 copy-start.2
  1.3 0.0 copy-start.3
  1.3 0.0 copy-start.4
  1.3 0.0 copy-start.5
  1.4 0.0 copy-start.6
  1.4 0.0 copy-start.7
  1.4 0.0 copy-start.8
  1.4 0.0 copy-start.9
  1.4 0.0 copy-start.10
  1.4 0.0 copy-start.11
  1.4 115.0 %step.1 = (bf16[2,960,128]{2,1,0:T(8,128)(2,1)S(1)}, f32[8,256]{1,0:T(8,128)S(1)}) custom-call(bf16[602,256]{1,0:T(8,128)(2,1)} %bitcast.15, bf16[2048,1024]{1,0:T(8,128)(2,1)} %adj_ref.1, s32[4,4]{1,0:T(4,128)} %occ_ref.1, s32[1,256]{1,0:T(1,128)} %bitcast.19, s32[1,256]{1,0:T(1,128)} %bitcast.20, s32[1]{0:T(128)S(6)} %copy.32.cnt_ref, f32[602,256]{1,0:T(8,128)} %refs_0_.1, ...), custom_call_target="tpu_custom_call" | custom-call | flops 6442450944 | bytes 4194304 | tf_op jit(solution)/shard_map/step/pallas_call | solution.py:1071
  116.4 0.0 copy-done
  116.4 0.0 copy-done.1
  116.4 0.0 copy-done.2
  116.4 0.0 copy-done.3
  116.4 0.0 copy-done.4
  116.5 0.0 copy-done.5
  116.5 0.0 copy-done.6
  116.5 0.0 copy-done.7
  116.5 0.0 copy-done.8
  116.5 0.0 copy-done.9
  116.5 2.2 %update.1 = (f32[602,256]{1,0:T(8,128)}, f32[602,256]{1,0:T(8,128)}, f32[602,256]{1,0:T(8,128)}, f32[256,256]{1,0:T(8,128)}, f32[256,256]{1,0:T(8,128)}, /*index...) custom-call(bf16[2,960,128]{2,1,0:T(8,128)(2,1)S(1)} %get-tuple-elem, ...), custom_call_target="tpu_custom_call" | custom-call | tf_op jit(solution)/shard_map/update/pallas_call | solution.py:1133
  (2 shorter events, 0.0 us)
Async XLA Ops:
  1.3 115.1 %copy-start = (f32[602,256]{1,0:T(8,128)S(1)}, f32[602,256]{1,0:T(8,128)}, u32[]{:S(2)}) copy-start(f32[602,256]{1,0:T(8,128)} %refs_0_.1) | copy-start | bytes 1849348
  1.3 115.1 %copy-start.1 = (f32[602,256]{1,0:T(8,128)S(1)}, f32[602,256]{1,0:T(8,128)}, u32[]{:S(2)}) copy-start(f32[602,256]{1,0:T(8,128)} %refs_1_.1) | copy-start | bytes 1849348
  1.3 115.1 %copy-start.2 = (f32[602,256]{1,0:T(8,128)S(1)}, f32[602,256]{1,0:T(8,128)}, u32[]{:S(2)}) copy-start(f32[602,256]{1,0:T(8,128)} %refs_2_.1) | copy-start | bytes 1849348
  1.3 115.1 %copy-start.3 = (f32[256,256]{1,0:T(8,128)S(1)}, f32[256,256]{1,0:T(8,128)}, u32[]{:S(2)}) copy-start(f32[256,256]{1,0:T(8,128)} %refs_3_.1) | copy-start | bytes 786436
  1.3 115.1 %copy-start.4 = (f32[256,256]{1,0:T(8,128)S(1)}, f32[256,256]{1,0:T(8,128)}, u32[]{:S(2)}) copy-start(f32[256,256]{1,0:T(8,128)} %refs_4_.1) | copy-start | bytes 786436
  1.3 115.1 %copy-start.5 = (f32[256,256]{1,0:T(8,128)S(1)}, f32[256,256]{1,0:T(8,128)}, u32[]{:S(2)}) copy-start(f32[256,256]{1,0:T(8,128)} %refs_5_.1) | copy-start | bytes 786436
  1.4 115.1 %copy-start.6 = (f32[256,41]{0,1:T(8,128)S(1)}, f32[256,41]{0,1:T(8,128)}, u32[]{:S(2)}) copy-start(f32[256,41]{0,1:T(8,128)} %param.26) | copy-start | bytes 125956
  1.4 115.1 %copy-start.7 = (f32[256,41]{0,1:T(8,128)S(1)}, f32[256,41]{0,1:T(8,128)}, u32[]{:S(2)}) copy-start(f32[256,41]{0,1:T(8,128)} %param.30) | copy-start | bytes 125956
  1.4 115.1 %copy-start.8 = (f32[256,41]{0,1:T(8,128)S(1)}, f32[256,41]{0,1:T(8,128)}, u32[]{:S(2)}) copy-start(f32[256,41]{0,1:T(8,128)} %param.34) | copy-start | bytes 125956
  1.4 115.1 %copy-start.9 = (f32[553]{0:T(1024)S(1)}, f32[553]{0:T(1024)}, u32[]{:S(2)}) copy-start(f32[553]{0:T(1024)} %refs_9_.1) | copy-start | bytes 6640
  1.4 115.1 %copy-start.10 = (f32[553]{0:T(1024)S(1)}, f32[553]{0:T(1024)}, u32[]{:S(2)}) copy-start(f32[553]{0:T(1024)} %refs_10_.1) | copy-start | bytes 6640
  1.4 115.1 %copy-start.11 = (f32[553]{0:T(1024)S(1)}, f32[553]{0:T(1024)}, u32[]{:S(2)}) copy-start(f32[553]{0:T(1024)} %refs_11_.1) | copy-start | bytes 6640

commit v7 on v6

--- a/solution.py
+++ b/solution.py
@@ -588,13 +588,13 @@
             own_parts.append(mine)
             pool[first, :, lane * (own // 2) : (lane + 1) * (own // 2)] = mine
             for q in (2 * lane, 2 * lane + 1):
+                to_x(0, q)
                 if relayed:
                     to_z(2, q)
                     to_z(1, q)
                 else:
                     for dz in range(nz - 1, 0, -1):
                         to_z(dz, q)
-                to_x(0, q)
 
         def source(dz, dx):
             return row_block(zback(dz) * nx + xs(nx - dx))
@@ -735,7 +735,7 @@
 
     lanes, plane = s.lanes, s.plane
     me = y * nx + x
-    others = [(dx, dy) for dx in range(nx) for dy in range(ny) if dx or dy]
+    others = [(dx, dy) for dx in range(nx - 1, -1, -1) for dy in range(ny - 1, -1, -1) if dx or dy]
 
     def lane_block(index):
         return pl.ds(pl.multiple_of(index * lanes, lanes), lanes)

time: 119 us -> 119 us (level)
  no operation moved by 1% of the time
where the time goes in v7:
time: 119 us
  Pallas kernels  117 us (98%)
  between operations  1.66 us (1%)
    pallas_call x1, Pallas kernels, shards(): pl.pallas_call(functools.partial(kernel, s), out_shape=(pltpu.VMEM((s.nk,...  115 us

profile of v7, /device:TPU:0, one launch (start us, length us, event | category | flops | bytes accessed | tf_op | source)
XLA Modules:
  0.0 118.5 jit_solution(4666895246960616913)
XLA Ops:
  1.3 0.0 copy-start
  1.3 0.0 copy-start.1
  1.3 0.0 copy-start.2
  1.3 0.0 copy-start.3
  1.3 0.0 copy-start.4
  1.3 0.0 copy-start.5
  1.4 0.0 copy-start.6
  1.4 0.0 copy-start.7
  1.4 0.0 copy-start.8
  1.4 0.0 copy-start.9
  1.4 0.0 copy-start.10
  1.4 0.0 copy-start.11
  1.4 114.7 %step.1 = (bf16[2,960,128]{2,1,0:T(8,128)(2,1)S(1)}, f32[8,256]{1,0:T(8,128)S(1)}) custom-call(bf16[602,256]{1,0:T(8,128)(2,1)} %bitcast.15, bf16[2048,1024]{1,0:T(8,128)(2,1)} %adj_ref.1, s32[4,4]{1,0:T(4,128)} %occ_ref.1, s32[1,256]{1,0:T(1,128)} %bitcast.19, s32[1,256]{1,0:T(1,128)} %bitcast.20, s32[1]{0:T(128)S(6)} %copy.32.cnt_ref, f32[602,256]{1,0:T(8,128)} %refs_0_.1, ...), custom_call_target="tpu_custom_call" | custom-call | flops 6442450944 | bytes 4194304 | tf_op jit(solution)/shard_map/step/pallas_call | solution.py:1071
  116.1 0.0 copy-done
  116.1 0.0 copy-done.1
  116.1 0.0 copy-done.2
  116.1 0.0 copy-done.3
  116.1 0.0 copy-done.4
  116.1 0.0 copy-done.5
  116.1 0.0 copy-done.6
  116.2 0.0 copy-done.7
  116.2 0.0 copy-done.8
  116.2 0.0 copy-done.9
  116.2 2.2 %update.1 = (f32[602,256]{1,0:T(8,128)}, f32[602,256]{1,0:T(8,128)}, f32[602,256]{1,0:T(8,128)}, f32[256,256]{1,0:T(8,128)}, f32[256,256]{1,0:T(8,128)}, /*index...) custom-call(bf16[2,960,128]{2,1,0:T(8,128)(2,1)S(1)} %get-tuple-elem, ...), custom_call_target="tpu_custom_call" | custom-call | tf_op jit(solution)/shard_map/update/pallas_call | solution.py:1133
  (2 shorter events, 0.0 us)
Async XLA Ops:
  1.3 114.8 %copy-start = (f32[602,256]{1,0:T(8,128)S(1)}, f32[602,256]{1,0:T(8,128)}, u32[]{:S(2)}) copy-start(f32[602,256]{1,0:T(8,128)} %refs_0_.1) | copy-start | bytes 1849348
  1.3 114.8 %copy-start.1 = (f32[602,256]{1,0:T(8,128)S(1)}, f32[602,256]{1,0:T(8,128)}, u32[]{:S(2)}) copy-start(f32[602,256]{1,0:T(8,128)} %refs_1_.1) | copy-start | bytes 1849348
  1.3 114.8 %copy-start.2 = (f32[602,256]{1,0:T(8,128)S(1)}, f32[602,256]{1,0:T(8,128)}, u32[]{:S(2)}) copy-start(f32[602,256]{1,0:T(8,128)} %refs_2_.1) | copy-start | bytes 1849348
  1.3 114.8 %copy-start.3 = (f32[256,256]{1,0:T(8,128)S(1)}, f32[256,256]{1,0:T(8,128)}, u32[]{:S(2)}) copy-start(f32[256,256]{1,0:T(8,128)} %refs_3_.1) | copy-start | bytes 786436
  1.3 114.8 %copy-start.4 = (f32[256,256]{1,0:T(8,128)S(1)}, f32[256,256]{1,0:T(8,128)}, u32[]{:S(2)}) copy-start(f32[256,256]{1,0:T(8,128)} %refs_4_.1) | copy-start | bytes 786436
  1.3 114.8 %copy-start.5 = (f32[256,256]{1,0:T(8,128)S(1)}, f32[256,256]{1,0:T(8,128)}, u32[]{:S(2)}) copy-start(f32[256,256]{1,0:T(8,128)} %refs_5_.1) | copy-start | bytes 786436
  1.4 114.8 %copy-start.6 = (f32[256,41]{0,1:T(8,128)S(1)}, f32[256,41]{0,1:T(8,128)}, u32[]{:S(2)}) copy-start(f32[256,41]{0,1:T(8,128)} %param.26) | copy-start | bytes 125956
  1.4 114.8 %copy-start.7 = (f32[256,41]{0,1:T(8,128)S(1)}, f32[256,41]{0,1:T(8,128)}, u32[]{:S(2)}) copy-start(f32[256,41]{0,1:T(8,128)} %param.30) | copy-start | bytes 125956
  1.4 114.8 %copy-start.8 = (f32[256,41]{0,1:T(8,128)S(1)}, f32[256,41]{0,1:T(8,128)}, u32[]{:S(2)}) copy-start(f32[256,41]{0,1:T(8,128)} %param.34) | copy-start | bytes 125956
  1.4 114.8 %copy-start.9 = (f32[553]{0:T(1024)S(1)}, f32[553]{0:T(1024)}, u32[]{:S(2)}) copy-start(f32[553]{0:T(1024)} %refs_9_.1) | copy-start | bytes 6640
  1.4 114.8 %copy-start.10 = (f32[553]{0:T(1024)S(1)}, f32[553]{0:T(1024)}, u32[]{:S(2)}) copy-start(f32[553]{0:T(1024)} %refs_10_.1) | copy-start | bytes 6640
  1.4 114.8 %copy-start.11 = (f32[553]{0:T(1024)S(1)}, f32[553]{0:T(1024)}, u32[]{:S(2)}) copy-start(f32[553]{0:T(1024)} %refs_11_.1) | copy-start | bytes 6640

commit v8 on v7

--- a/solution.py
+++ b/solution.py
@@ -286,7 +286,7 @@
         if nk > 1:
             send(mine, mine, gbase[hop] + c * nh + q, sibling)
 
-    def complete_gather(hop):
+    def complete_gather(hop, meanwhile):
         for q in range(nh):
             for d in range(1, ny):
                 source = ys(ny - d) * nk + k
@@ -294,13 +294,12 @@
                 arrived(block, gbase[hop] + source * nh + q)
                 if nk > 1:
                     send(block, block, gbase[hop] + source * nh + q, sibling)
-        if nk > 1:
+        for d in range(ny if nk > 1 else 0):
+            if d == 1:
+                meanwhile()
+            source = ys(d) * nk + 1 - k
             for q in range(nh):
-                for d in range(ny):
-                    source = ys(d) * nk + 1 - k
-                    arrived(
-                        v_all.at[hop, row_part(source, q)], gbase[hop] + source * nh + q
-                    )
+                arrived(v_all.at[hop, row_part(source, q)], gbase[hop] + source * nh + q)
 
     with jax.named_scope("barrier"):
         pl.semaphore_wait(barrier, len(peers))
@@ -325,8 +324,24 @@
 
     def spread(hop, finish):
         settle(of="hop")
+        start_z = nz - 1
+        begun = []
+        late = [ys(d) * nk + 1 - k for d in range(1, ny)] if nk > 1 else []
+        soon = [ys(d) * nk + k for d in range(ny)] + ([y * nk + 1 - k] if nk > 1 else [])
+
+        def some(sources):
+            first_rows = row_block(zs(start_z) * nx + xs(1))
+            total = None
+            for source in sources:
+                here = dot(
+                    tile[first_rows, row_block(source)], v_all[hop, row_block(source), :]
+                )
+                total = here if total is None else total + here
+            return total
+
+        split = nx > 1 and nk > 1 and ny > 1
         with jax.named_scope("gather_y"):
-            complete_gather(hop)
+            complete_gather(hop, lambda: begun.append(some(soon)) if split else None)
         zbase = wide[hop]
         xbase = zbase + nz * nh
         order = list(range(nz - 1, -1, -1))
@@ -357,9 +372,11 @@
                     if (dz, dx) not in ready:
                         ready.add((dz, dx))
                         rt = zs(dz) * nx + xs(dx)
-                        xsend[(dx - 1) * nz + dz] = dot(
-                            tile[row_block(rt), :], v_all[hop]
-                        ).astype(LOW)
+                        if split and (dz, dx) == (start_z, 1):
+                            here = begun[0] + some(late)
+                        else:
+                            here = dot(tile[row_block(rt), :], v_all[hop])
+                        xsend[(dx - 1) * nz + dz] = here.astype(LOW)
                     send_x(dz, dx, q)
             for dz in order:
                 acc[:, dz * own : (dz + 1) * own] = dot(

time: 119 us -> 119 us (level)
  no operation moved by 1% of the time
where the time goes in v8:
time: 119 us; the launch traced here: 118 us
  Pallas kernels  117 us (98%)
  between operations  1.66 us (1%)
    pallas_call x1, Pallas kernels, shards(): pl.pallas_call(functools.partial(kernel, s), out_shape=(pltpu.VMEM((s.nk,...  115 us

profile of v8, /device:TPU:0, one launch (start us, length us, event | category | flops | bytes accessed | tf_op | source)
XLA Modules:
  0.0 118.4 jit_solution(16483157566114318874)
XLA Ops:
  1.3 0.0 copy-start
  1.3 0.0 copy-start.1
  1.3 0.0 copy-start.2
  1.3 0.0 copy-start.3
  1.3 0.0 copy-start.4
  1.3 0.0 copy-start.5
  1.4 0.0 copy-start.6
  1.4 0.0 copy-start.7
  1.4 0.0 copy-start.8
  1.4 0.0 copy-start.9
  1.4 0.0 copy-start.10
  1.4 0.0 copy-start.11
  1.4 114.6 %step.1 = (bf16[2,960,128]{2,1,0:T(8,128)(2,1)S(1)}, f32[8,256]{1,0:T(8,128)S(1)}) custom-call(bf16[602,256]{1,0:T(8,128)(2,1)} %bitcast.15, bf16[2048,1024]{1,0:T(8,128)(2,1)} %adj_ref.1, s32[4,4]{1,0:T(4,128)} %occ_ref.1, s32[1,256]{1,0:T(1,128)} %bitcast.19, s32[1,256]{1,0:T(1,128)} %bitcast.20, s32[1]{0:T(128)S(6)} %copy.32.cnt_ref, f32[602,256]{1,0:T(8,128)} %refs_0_.1, ...), custom_call_target="tpu_custom_call" | custom-call | flops 6442450944 | bytes 4194304 | tf_op jit(solution)/shard_map/step/pallas_call | solution.py:1088
  116.0 0.0 copy-done
  116.0 0.0 copy-done.1
  116.0 0.0 copy-done.2
  116.0 0.0 copy-done.3
  116.0 0.0 copy-done.4
  116.0 0.0 copy-done.5
  116.0 0.0 copy-done.6
  116.1 0.0 copy-done.7
  116.1 0.0 copy-done.8
  116.1 0.0 copy-done.9
  116.1 2.2 %update.1 = (f32[602,256]{1,0:T(8,128)}, f32[602,256]{1,0:T(8,128)}, f32[602,256]{1,0:T(8,128)}, f32[256,256]{1,0:T(8,128)}, f32[256,256]{1,0:T(8,128)}, /*index...) custom-call(bf16[2,960,128]{2,1,0:T(8,128)(2,1)S(1)} %get-tuple-elem, ...), custom_call_target="tpu_custom_call" | custom-call | tf_op jit(solution)/shard_map/update/pallas_call | solution.py:1150
  (2 shorter events, 0.0 us)
Async XLA Ops:
  1.3 114.7 %copy-start = (f32[602,256]{1,0:T(8,128)S(1)}, f32[602,256]{1,0:T(8,128)}, u32[]{:S(2)}) copy-start(f32[602,256]{1,0:T(8,128)} %refs_0_.1) | copy-start | bytes 1849348
  1.3 114.7 %copy-start.1 = (f32[602,256]{1,0:T(8,128)S(1)}, f32[602,256]{1,0:T(8,128)}, u32[]{:S(2)}) copy-start(f32[602,256]{1,0:T(8,128)} %refs_1_.1) | copy-start | bytes 1849348
  1.3 114.7 %copy-start.2 = (f32[602,256]{1,0:T(8,128)S(1)}, f32[602,256]{1,0:T(8,128)}, u32[]{:S(2)}) copy-start(f32[602,256]{1,0:T(8,128)} %refs_2_.1) | copy-start | bytes 1849348
  1.3 114.7 %copy-start.3 = (f32[256,256]{1,0:T(8,128)S(1)}, f32[256,256]{1,0:T(8,128)}, u32[]{:S(2)}) copy-start(f32[256,256]{1,0:T(8,128)} %refs_3_.1) | copy-start | bytes 786436
  1.3 114.7 %copy-start.4 = (f32[256,256]{1,0:T(8,128)S(1)}, f32[256,256]{1,0:T(8,128)}, u32[]{:S(2)}) copy-start(f32[256,256]{1,0:T(8,128)} %refs_4_.1) | copy-start | bytes 786436
  1.3 114.7 %copy-start.5 = (f32[256,256]{1,0:T(8,128)S(1)}, f32[256,256]{1,0:T(8,128)}, u32[]{:S(2)}) copy-start(f32[256,256]{1,0:T(8,128)} %refs_5_.1) | copy-start | bytes 786436
  1.4 114.7 %copy-start.6 = (f32[256,41]{0,1:T(8,128)S(1)}, f32[256,41]{0,1:T(8,128)}, u32[]{:S(2)}) copy-start(f32[256,41]{0,1:T(8,128)} %param.26) | copy-start | bytes 125956
  1.4 114.7 %copy-start.7 = (f32[256,41]{0,1:T(8,128)S(1)}, f32[256,41]{0,1:T(8,128)}, u32[]{:S(2)}) copy-start(f32[256,41]{0,1:T(8,128)} %param.30) | copy-start | bytes 125956
  1.4 114.7 %copy-start.8 = (f32[256,41]{0,1:T(8,128)S(1)}, f32[256,41]{0,1:T(8,128)}, u32[]{:S(2)}) copy-start(f32[256,41]{0,1:T(8,128)} %param.34) | copy-start | bytes 125956
  1.4 114.7 %copy-start.9 = (f32[553]{0:T(1024)S(1)}, f32[553]{0:T(1024)}, u32[]{:S(2)}) copy-start(f32[553]{0:T(1024)} %refs_9_.1) | copy-start | bytes 6640
  1.4 114.7 %copy-start.10 = (f32[553]{0:T(1024)S(1)}, f32[553]{0:T(1024)}, u32[]{:S(2)}) copy-start(f32[553]{0:T(1024)} %refs_10_.1) | copy-start | bytes 6640
  1.4 114.7 %copy-start.11 = (f32[553]{0:T(1024)S(1)}, f32[553]{0:T(1024)}, u32[]{:S(2)}) copy-start(f32[553]{0:T(1024)} %refs_11_.1) | copy-start | bytes 6640

commit v9 on v8

--- a/solution.py
+++ b/solution.py
@@ -444,28 +444,27 @@
             sum_z(nh - 1)
 
     bias = [bias_ref[i * width : (i + 1) * width].reshape(1, width) for i in range(2)]
-    slopes, acts = [None] * nh, [None] * nh
+    acts = [None] * nh
 
     def first_done(q, total):
         rows_q = span_of(q)
         z1 = total + v_all[0, row_part(c, q), :].astype(FULL) + bias[0]
-        act, slope = gelu_both(z1)
-        h1 = act.astype(LOW) * valid_low[rows_q]
+        h1 = gelu_both(z1)[0].astype(LOW) * valid_low[rows_q]
         start_gather(1, q, dot(h1, w2).astype(LOW))
-        acts[q], slopes[q] = h1, slope * valid_col[rows_q]
+        acts[q] = h1
+        acc[rows_q, :width] = z1
 
     spread(0, first_done)
     h1t = jnp.concatenate(acts, axis=0).astype(FULL).T.astype(LOW)
-    slope1t = jnp.concatenate(slopes, axis=0).T
+    slope1t = (gelu_both(acc[:, :width])[1] * valid_col).T
 
     xt_base = gbase[1] + s.n_col
 
     def second_done(q, total):
         rows_q = span_of(q)
         z2 = total + v_all[1, row_part(c, q), :].astype(FULL) + bias[1]
-        act, slope = gelu_both(z2)
-        acts[q] = act.astype(LOW) * valid_low[rows_q]
-        slopes[q] = slope * valid_col[rows_q]
+        acts[q] = gelu_both(z2)[0].astype(LOW) * valid_low[rows_q]
+        acc[rows_q, :width] = z2
         ends = span_of(q).stop
         if ends % (own // 2) == 0:
             lane = 2 * ends // own - 1
@@ -484,7 +483,7 @@
     h2 = jnp.concatenate(acts, axis=0)
 
     with jax.named_scope("hop3_gather"):
-        slope2t = jnp.concatenate(slopes, axis=0).T
+        slope2t = (gelu_both(acc[:, :width])[1] * valid_col).T
         settle(s.n_col - 1)
         for lane in range(2):
             for dy, dk in reversed(col_far):

time: 119 us -> 119 us (level)
  no operation moved by 1% of the time
where the time goes in v9:
time: 119 us; the launch traced here: 118 us
  Pallas kernels  117 us (98%)
  between operations  1.66 us (1%)
    pallas_call x1, Pallas kernels, shards(): pl.pallas_call(functools.partial(kernel, s), out_shape=(pltpu.VMEM((s.nk,...  115 us

profile of v9, /device:TPU:0, one launch (start us, length us, event | category | flops | bytes accessed | tf_op | source)
XLA Modules:
  0.0 118.4 jit_solution(10871197940746761768)
XLA Ops:
  1.3 0.0 copy-start
  1.3 0.0 copy-start.1
  1.3 0.0 copy-start.2
  1.3 0.0 copy-start.3
  1.3 0.0 copy-start.4
  1.3 0.0 copy-start.5
  1.4 0.0 copy-start.6
  1.4 0.0 copy-start.7
  1.4 0.0 copy-start.8
  1.4 0.0 copy-start.9
  1.4 114.5 %step.1 = (bf16[2,960,128]{2,1,0:T(8,128)(2,1)S(1)}, f32[8,256]{1,0:T(8,128)S(1)}) custom-call(bf16[602,256]{1,0:T(8,128)(2,1)} %bitcast.15, bf16[2048,1024]{1,0:T(8,128)(2,1)} %adj_ref.1, s32[4,4]{1,0:T(4,128)} %occ_ref.1, s32[1,256]{1,0:T(1,128)} %bitcast.19, s32[1,256]{1,0:T(1,128)} %bitcast.20, s32[1]{0:T(128)S(6)} %copy.32.cnt_ref, f32[602,256]{1,0:T(8,128)} %refs_0_.1, ...), custom_call_target="tpu_custom_call" | custom-call | flops 6442450944 | bytes 4194304 | tf_op jit(solution)/shard_map/step/pallas_call | solution.py:1087
  115.9 0.0 copy-done
  115.9 0.0 copy-done.1
  116.0 0.0 copy-done.2
  116.0 0.0 copy-done.3
  116.0 0.0 copy-done.4
  116.0 0.0 copy-done.5
  116.0 0.0 copy-done.6
  116.0 0.0 copy-done.7
  116.0 0.0 copy-done.8
  116.0 0.0 copy-done.9
  116.0 0.0 copy-done.10
  116.0 0.0 copy-done.11
  116.1 2.2 %update.1 = (f32[602,256]{1,0:T(8,128)}, f32[602,256]{1,0:T(8,128)}, f32[602,256]{1,0:T(8,128)}, f32[256,256]{1,0:T(8,128)}, f32[256,256]{1,0:T(8,128)}, /*index...) custom-call(bf16[2,960,128]{2,1,0:T(8,128)(2,1)S(1)} %get-tuple-elem, ...), custom_call_target="tpu_custom_call" | custom-call | tf_op jit(solution)/shard_map/update/pallas_call | solution.py:1149
  (2 shorter events, 0.0 us)
Async XLA Ops:
  1.3 114.6 %copy-start = (f32[602,256]{1,0:T(8,128)S(1)}, f32[602,256]{1,0:T(8,128)}, u32[]{:S(2)}) copy-start(f32[602,256]{1,0:T(8,128)} %refs_0_.1) | copy-start | bytes 1849348
  1.3 114.6 %copy-start.1 = (f32[602,256]{1,0:T(8,128)S(1)}, f32[602,256]{1,0:T(8,128)}, u32[]{:S(2)}) copy-start(f32[602,256]{1,0:T(8,128)} %refs_1_.1) | copy-start | bytes 1849348
  1.3 114.6 %copy-start.2 = (f32[602,256]{1,0:T(8,128)S(1)}, f32[602,256]{1,0:T(8,128)}, u32[]{:S(2)}) copy-start(f32[602,256]{1,0:T(8,128)} %refs_2_.1) | copy-start | bytes 1849348
  1.3 114.6 %copy-start.3 = (f32[256,256]{1,0:T(8,128)S(1)}, f32[256,256]{1,0:T(8,128)}, u32[]{:S(2)}) copy-start(f32[256,256]{1,0:T(8,128)} %refs_3_.1) | copy-start | bytes 786436
  1.3 114.6 %copy-start.4 = (f32[256,256]{1,0:T(8,128)S(1)}, f32[256,256]{1,0:T(8,128)}, u32[]{:S(2)}) copy-start(f32[256,256]{1,0:T(8,128)} %refs_4_.1) | copy-start | bytes 786436
  1.3 114.6 %copy-start.5 = (f32[256,256]{1,0:T(8,128)S(1)}, f32[256,256]{1,0:T(8,128)}, u32[]{:S(2)}) copy-start(f32[256,256]{1,0:T(8,128)} %refs_5_.1) | copy-start | bytes 786436
  1.4 114.6 %copy-start.6 = (f32[256,41]{0,1:T(8,128)S(1)}, f32[256,41]{0,1:T(8,128)}, u32[]{:S(2)}) copy-start(f32[256,41]{0,1:T(8,128)} %param.26) | copy-start | bytes 125956
  1.4 114.6 %copy-start.7 = (f32[256,41]{0,1:T(8,128)S(1)}, f32[256,41]{0,1:T(8,128)}, u32[]{:S(2)}) copy-start(f32[256,41]{0,1:T(8,128)} %param.30) | copy-start | bytes 125956
  1.4 114.6 %copy-start.8 = (f32[256,41]{0,1:T(8,128)S(1)}, f32[256,41]{0,1:T(8,128)}, u32[]{:S(2)}) copy-start(f32[256,41]{0,1:T(8,128)} %param.34) | copy-start | bytes 125956
  1.4 114.6 %copy-start.9 = (f32[553]{0:T(1024)S(1)}, f32[553]{0:T(1024)}, u32[]{:S(2)}) copy-start(f32[553]{0:T(1024)} %refs_9_.1) | copy-start | bytes 6640
  1.4 114.6 %copy-start.10 = (f32[553]{0:T(1024)S(1)}, f32[553]{0:T(1024)}, u32[]{:S(2)}) copy-start(f32[553]{0:T(1024)} %refs_10_.1) | copy-start | bytes 6640
  1.4 114.6 %copy-start.11 = (f32[553]{0:T(1024)S(1)}, f32[553]{0:T(1024)}, u32[]{:S(2)}) copy-start(f32[553]{0:T(1024)} %refs_11_.1) | copy-start | bytes 6640
